TPU v7x, 128 devices: a whole 4x4x4 slice. The times are simulated.
128 devices in a mesh: dp: 8 (over x_lo, y), grp: 16 (over x_hi, z, core).
Axes of the slice: x: 4 (x_hi: 2, x_lo: 2; x = x_hi * 2 + x_lo), y: 4, z: 4, core: 2. Of those that a mesh axis runs over, the one named last changes fastest.
Arguments:
- tokens: bfloat16 [64, 1024, 512], P('dp', 'grp'), may hold values from -6 to 6
- cotangent: bfloat16 [64, 1024, 512], P('dp', 'grp'), may hold values from -6 to 6
- w_qkv: bfloat16 [512, 1536], replicated, may hold values from -0.25 to 0.25
- w_out: bfloat16 [512, 512], replicated, may hold values from -1.5 to 1.5
- gain_attn: float32 [512], replicated, may hold values from 0.5 to 1.5
- gain_mix: float32 [512], replicated, may hold values from 0.5 to 1.5
- w_ctrl: bfloat16 [512, 16], replicated, may hold values from -0.125 to 0.125
- w_in: bfloat16 [16, 512, 2048], P('grp'), may hold values from -1.5 to 1.5
- w_back: bfloat16 [16, 2048, 512], P('grp'), may hold values from -1.5 to 1.5
- prefix: int32 [64], P('dp'), may hold values from 102 to 512
- group_ids: int32 [64, 1024], P('dp', 'grp'), may hold values from 0 to 1, as said below
Outputs:
- tokens_out: bfloat16 [64, 1024, 512], P('dp', 'grp')
- token_grad: float32 [64, 1024, 512], P('dp', 'grp')
- grad_qkv: float32 [512, 1536], replicated
- grad_out: float32 [512, 512], replicated
- grad_gain_attn: float32 [512], replicated
- grad_gain_mix: float32 [512], replicated
- grad_ctrl: float32 [512, 16], replicated
- grad_in: float32 [16, 512, 2048], P('grp')
- grad_back: float32 [16, 2048, 512], P('grp')
Inputs may be any that keep to these rules, and one draw needn't show every extreme that they name: `group_ids`: in each sequence, every aligned block of 64 positions holds exactly 32 positions of each id.
All inputs are finite; a program needn't handle non-finite values.
Results may differ from a plain program's by a relative error of at most 0.02.
Values may be sent and summed in bfloat16 or wider, within the bound.
A program may use at most 128 MiB of HBM per device.

v0:
```python
import jax
import jax.numpy as jnp
from jax import lax
from jax.sharding import PartitionSpec as P

HEADS = 8
HEAD_DIM = 64
GROUP = 32
BLOCK = 64


EPSILON = 1e-05
MASKED = -1e30


def norm_forward(seq_rows, gain_vec):
    row_mean = jnp.mean(seq_rows, axis=-1, keepdims=True)
    centred = seq_rows - row_mean
    inv_std = lax.rsqrt(jnp.mean(centred * centred, axis=-1, keepdims=True) + EPSILON)
    unit_rows = centred * inv_std
    return (unit_rows * gain_vec, unit_rows, inv_std)


def norm_backward(upstream, unit_rows, inv_std, gain_vec):
    grad_unit = upstream * gain_vec
    centred_grad = (
        grad_unit
        - jnp.mean(grad_unit, axis=-1, keepdims=True)
        - unit_rows * jnp.mean(grad_unit * unit_rows, axis=-1, keepdims=True)
    )
    return (inv_std * centred_grad, jnp.sum(upstream * unit_rows, axis=0))


def masked_scores(queries, keys_in, query_pos, key_pos, prefix_len):
    factor = queries.shape[-1] ** (-0.5)
    product = (
        jnp.einsum("qhd,khd->hqk", queries, keys_in, preferred_element_type=jnp.float32) * factor
    )
    visible = (key_pos[None, :] <= query_pos[:, None]) | (key_pos[None, :] < prefix_len)
    return jnp.where(visible[None], product, MASKED)


def mixing_weights(resid, id_rows, gain_mix, w_ctrl):
    blocks = resid.shape[0] // BLOCK
    per_block = BLOCK // GROUP
    normed, unit_rows, inv_std = norm_forward(resid, gain_mix)
    mix_in = normed.astype(jnp.bfloat16)
    logits = jnp.dot(mix_in, w_ctrl, preferred_element_type=jnp.float32)
    member = (
        id_rows.reshape(blocks, BLOCK)[..., None] == jnp.arange(per_block, dtype=jnp.int32)
    ).astype(jnp.float32)
    blocked = logits.reshape(blocks, BLOCK, logits.shape[1])
    exponent = jnp.exp(blocked - jnp.max(blocked, axis=1, keepdims=True))
    totals = jnp.einsum("nbg,nbe->nge", member, exponent, precision=lax.Precision.HIGHEST)
    weights = exponent / jnp.einsum("nbg,nge->nbe", member, totals, precision=lax.Precision.HIGHEST)
    mix_coef = member.astype(jnp.bfloat16)[..., None] * weights.astype(jnp.bfloat16)[:, :, None, :]
    return (mix_in, unit_rows, inv_std, member, weights, mix_coef)


def on_device(
    tokens, cotangent, w_qkv, w_out, gain_attn, gain_mix, w_ctrl, w_in, w_back, prefix, group_ids
):
    local_len = tokens.shape[1]
    model_width = tokens.shape[2]
    num_experts = w_ctrl.shape[1]
    blocks = local_len // BLOCK
    per_block = BLOCK // GROUP
    group_count = blocks * per_block
    full_len = local_len * lax.axis_size("grp")
    factor = HEAD_DIM ** (-0.5)
    query_pos = lax.axis_index("grp") * local_len + jnp.arange(local_len, dtype=jnp.int32)
    key_pos = jnp.arange(full_len, dtype=jnp.int32)

    def forward_step(running, inputs):
        seq_rows, prefix_len, id_rows = inputs
        rows_float = seq_rows.astype(jnp.float32)
        normed, unit_attn, inv_attn = norm_forward(rows_float, gain_attn)
        attn_in = normed.astype(jnp.bfloat16)
        projected = jnp.dot(attn_in, w_qkv, preferred_element_type=jnp.float32).astype(jnp.bfloat16)
        keys_vals = lax.all_gather(projected[:, model_width:], "grp", axis=0, tiled=True)
        queries = projected[:, :model_width].reshape(local_len, HEADS, HEAD_DIM)
        keys_all = keys_vals[:, :model_width].reshape(full_len, HEADS, HEAD_DIM)
        values_all = keys_vals[:, model_width:].reshape(full_len, HEADS, HEAD_DIM)
        scores = masked_scores(queries, keys_all, query_pos, key_pos, prefix_len)
        row_top = jnp.max(scores, axis=-1, keepdims=True)
        exponent = jnp.exp(scores - row_top)
        totals = jnp.sum(exponent, axis=-1, keepdims=True)
        attn_probs = exponent / totals
        log_total = (row_top + jnp.log(totals))[..., 0]
        attn_mix = jnp.einsum(
            "hqk,khd->qhd",
            attn_probs.astype(jnp.bfloat16),
            values_all,
            preferred_element_type=jnp.float32,
        )
        attn_mix = attn_mix.reshape(local_len, model_width).astype(jnp.bfloat16)
        resid = rows_float + jnp.dot(attn_mix, w_out, preferred_element_type=jnp.float32)
        mix_in, unit_mix, inv_mix, member, weights, mix_coef = mixing_weights(
            resid, id_rows, gain_mix, w_ctrl
        )
        mixed = jnp.einsum(
            "nbge,nbd->nged",
            mix_coef,
            mix_in.reshape(blocks, BLOCK, model_width),
            preferred_element_type=jnp.float32,
        )
        mixed = mixed.reshape(group_count, num_experts, model_width).astype(jnp.bfloat16)
        at_owner = lax.all_to_all(mixed, "grp", split_axis=1, concat_axis=0, tiled=True)
        pre_act = jnp.einsum("ged,edf->gef", at_owner, w_in, preferred_element_type=jnp.float32)
        hidden = jax.nn.silu(pre_act).astype(jnp.bfloat16)
        expert_out = jnp.einsum(
            "gef,efd->ged", hidden, w_back, preferred_element_type=jnp.float32
        ).astype(jnp.bfloat16)
        returned = lax.all_to_all(
            expert_out, "grp", split_axis=0, concat_axis=1, tiled=True
        ).reshape(blocks, per_block, num_experts, model_width)
        branch = jnp.einsum(
            "nbge,nged->nbd", mix_coef, returned, preferred_element_type=jnp.float32
        ).reshape(local_len, model_width)
        kept_kv = keys_vals[:0]
        residues = (resid, log_total, attn_mix, projected, at_owner, pre_act, returned, kept_kv)
        return (running, ((resid + branch).astype(jnp.bfloat16), residues))

    unused, (tokens_out, residues) = lax.scan(forward_step, None, (tokens, prefix, group_ids))

    def backward_step(running, inputs):
        seq_rows, grad_rows, prefix_len, id_rows, kept = inputs
        resid, log_total, attn_mix, projected, at_owner, pre_act, returned, kept_kv = kept
        acc_qkv, acc_out, acc_gain_attn, acc_gain_mix, acc_ctrl, acc_in, acc_back = running
        normed, unit_attn, inv_attn = norm_forward(seq_rows.astype(jnp.float32), gain_attn)
        attn_in = normed.astype(jnp.bfloat16)
        mix_in, unit_mix, inv_mix, member, weights, mix_coef = mixing_weights(
            resid, id_rows, gain_mix, w_ctrl
        )
        grad_blocks = grad_rows.reshape(blocks, BLOCK, model_width)
        grad_coef = jnp.einsum(
            "nbd,nged->nbge", grad_blocks, returned, preferred_element_type=jnp.float32
        )
        grad_expert = jnp.einsum(
            "nbge,nbd->nged", mix_coef, grad_blocks, preferred_element_type=jnp.float32
        )
        grad_expert = grad_expert.reshape(group_count, num_experts, model_width).astype(
            jnp.bfloat16
        )
        grad_owner = lax.all_to_all(grad_expert, "grp", split_axis=1, concat_axis=0, tiled=True)
        hidden = jax.nn.silu(pre_act).astype(jnp.bfloat16)
        grad_hidden = jnp.einsum(
            "ged,efd->gef", grad_owner, w_back, preferred_element_type=jnp.float32
        ).astype(jnp.bfloat16)
        sigmoid_pre = jax.nn.sigmoid(pre_act)
        slope = sigmoid_pre * (1.0 + pre_act * (1.0 - sigmoid_pre))
        grad_pre = (grad_hidden.astype(jnp.float32) * slope).astype(jnp.bfloat16)
        acc_back = acc_back + jnp.einsum(
            "gef,ged->efd", hidden, grad_owner, preferred_element_type=jnp.float32
        )
        acc_in = acc_in + jnp.einsum(
            "ged,gef->edf", at_owner, grad_pre, preferred_element_type=jnp.float32
        )
        grad_mixed = jnp.einsum(
            "gef,edf->ged", grad_pre, w_in, preferred_element_type=jnp.float32
        ).astype(jnp.bfloat16)
        grad_home = lax.all_to_all(
            grad_mixed, "grp", split_axis=0, concat_axis=1, tiled=True
        ).reshape(blocks, per_block, num_experts, model_width)
        mix_blocks = mix_in.reshape(blocks, BLOCK, model_width)
        grad_coef = grad_coef + jnp.einsum(
            "nged,nbd->nbge", grad_home, mix_blocks, preferred_element_type=jnp.float32
        )
        grad_mix_in = jnp.einsum(
            "nbge,nged->nbd", mix_coef, grad_home, preferred_element_type=jnp.float32
        ).reshape(local_len, model_width)
        grad_weights = jnp.einsum(
            "nbg,nbge->nbe", member, grad_coef, precision=lax.Precision.HIGHEST
        )
        group_dot = jnp.einsum(
            "nbg,nbe->nge", member, weights * grad_weights, precision=lax.Precision.HIGHEST
        )
        spread_back = jnp.einsum("nbg,nge->nbe", member, group_dot, precision=lax.Precision.HIGHEST)
        grad_logits = (
            (weights * (grad_weights - spread_back))
            .reshape(local_len, num_experts)
            .astype(jnp.bfloat16)
        )
        acc_ctrl = acc_ctrl + jnp.einsum(
            "pd,pe->de", mix_in, grad_logits, preferred_element_type=jnp.float32
        )
        grad_mix_in = grad_mix_in + jnp.dot(
            grad_logits, w_ctrl.T, preferred_element_type=jnp.float32
        )
        grad_norm_mix, gain_mix_part = norm_backward(grad_mix_in, unit_mix, inv_mix, gain_mix)
        grad_resid = grad_rows.astype(jnp.float32) + grad_norm_mix
        grad_branch = grad_resid.astype(jnp.bfloat16)
        acc_out = acc_out + jnp.einsum(
            "pd,pe->de", attn_mix, grad_branch, preferred_element_type=jnp.float32
        )
        grad_attn_mix = jnp.dot(grad_branch, w_out.T, preferred_element_type=jnp.float32).astype(
            jnp.bfloat16
        )
        keys_vals = lax.all_gather(projected[:, model_width:], "grp", axis=0, tiled=True)
        queries = projected[:, :model_width].reshape(local_len, HEADS, HEAD_DIM)
        keys_all = keys_vals[:, :model_width].reshape(full_len, HEADS, HEAD_DIM)
        values_all = keys_vals[:, model_width:].reshape(full_len, HEADS, HEAD_DIM)
        scores = masked_scores(queries, keys_all, query_pos, key_pos, prefix_len)
        attn_probs = jnp.exp(scores - log_total[..., None])
        grad_heads = grad_attn_mix.reshape(local_len, HEADS, HEAD_DIM)
        grad_probs = jnp.einsum(
            "qhd,khd->hqk", grad_heads, values_all, preferred_element_type=jnp.float32
        )
        inner_sum = jnp.sum(attn_probs * grad_probs, axis=-1)
        grad_scores = (attn_probs * (grad_probs - inner_sum[..., None])).astype(jnp.bfloat16)
        grad_queries = (
            jnp.einsum("hqk,khd->qhd", grad_scores, keys_all, preferred_element_type=jnp.float32)
            * factor
        )
        grad_queries = grad_queries.reshape(local_len, model_width).astype(jnp.bfloat16)
        key_terms = (
            jnp.einsum("hqk,qhd->khd", grad_scores, queries, preferred_element_type=jnp.float32)
            * factor
        ).reshape(full_len, model_width)
        value_terms = jnp.einsum(
            "hqk,qhd->khd",
            attn_probs.astype(jnp.bfloat16),
            grad_heads,
            preferred_element_type=jnp.float32,
        ).reshape(full_len, model_width)
        grad_keys, grad_values = (
            lax.psum_scatter(
                key_terms.astype(jnp.bfloat16), "grp", scatter_dimension=0, tiled=True
            ).astype(jnp.float32),
            lax.psum_scatter(
                value_terms.astype(jnp.bfloat16), "grp", scatter_dimension=0, tiled=True
            ).astype(jnp.float32),
        )
        grad_act = jnp.concatenate(
            [grad_queries, grad_keys.astype(jnp.bfloat16), grad_values.astype(jnp.bfloat16)], axis=1
        )
        acc_qkv = acc_qkv + jnp.einsum(
            "pd,pe->de", attn_in, grad_act, preferred_element_type=jnp.float32
        )
        grad_attn_in = jnp.dot(grad_act, w_qkv.T, preferred_element_type=jnp.float32)
        grad_norm_attn, gain_attn_part = norm_backward(grad_attn_in, unit_attn, inv_attn, gain_attn)
        running = (
            acc_qkv,
            acc_out,
            acc_gain_attn + gain_attn_part,
            acc_gain_mix + gain_mix_part,
            acc_ctrl,
            acc_in,
            acc_back,
        )
        return (running, grad_resid + grad_norm_attn)

    start_grads = (
        jnp.zeros(w_qkv.shape, jnp.float32),
        jnp.zeros(w_out.shape, jnp.float32),
        jnp.zeros(gain_attn.shape, jnp.float32),
        jnp.zeros(gain_mix.shape, jnp.float32),
        jnp.zeros(w_ctrl.shape, jnp.float32),
        jnp.zeros(w_in.shape, jnp.float32),
        jnp.zeros(w_back.shape, jnp.float32),
    )
    summed, token_grad = lax.scan(
        backward_step, start_grads, (tokens, cotangent, prefix, group_ids, residues)
    )
    acc_qkv, acc_out, acc_gain_attn, acc_gain_mix, acc_ctrl, acc_in, acc_back = summed
    grad_in, grad_back = (
        lax.psum(acc_in.astype(jnp.bfloat16), "dp").astype(jnp.float32),
        lax.psum(acc_back.astype(jnp.bfloat16), "dp").astype(jnp.float32),
    )
    grad_qkv, grad_out, grad_gain_attn, grad_gain_mix, grad_ctrl = lax.psum(
        (acc_qkv, acc_out, acc_gain_attn, acc_gain_mix, acc_ctrl), ("dp", "grp")
    )
    return (
        tokens_out,
        token_grad,
        grad_qkv,
        grad_out,
        grad_gain_attn,
        grad_gain_mix,
        grad_ctrl,
        grad_in,
        grad_back,
    )


def solution(mesh):
    in_specs = (
        P("dp", "grp", None),
        P("dp", "grp", None),
        P(),
        P(),
        P(),
        P(),
        P(),
        P("grp", None, None),
        P("grp", None, None),
        P("dp"),
        P("dp", "grp"),
    )
    out_specs = (
        P("dp", "grp", None),
        P("dp", "grp", None),
        P(),
        P(),
        P(),
        P(),
        P(),
        P("grp", None, None),
        P("grp", None, None),
    )
    return jax.shard_map(
        on_device, mesh=mesh, in_specs=in_specs, out_specs=out_specs, check_vma=False
    )
```

profile of v0, /device:TPU:1, one launch (start us, length us, event | category | flops | bytes accessed | tf_op | source)
XLA Modules:
  0.0 2635.5 jit_solution(4599333925492079110)
XLA Ops:
  9.2 712.1 %while.52 = (s32[]{:T(128)}, bf16[8,64,512]{2,1,0:T(8,128)(2,1)}, f32[8,64,512]{2,1,0:T(8,128)}, f32[8,8,64]{2,1,0:T(8,128)}, bf16[8,64,512]{2,1,0:T(8,128)(2,1)...) while((s32[]{:T(128)}, bf16[8,64,512]{2,1,0:T(8,128)(2,1)}, ...), condition=%wide.region_8.9_spmd.clone.clone, body=%wide.region_0.8_spmd.clone.clone.sunk | while | flops 415623488 | bytes 57683080 | solution.py:124
  16.8 49.1 %all-gather.3.cloned.1.call-done = bf16[1024,1024]{1,0:T(8,128)(2,1)} async-done(((bf16[64,1024]{1,0:T(8,128)(2,1)}), bf16[1024,1024]{1,0:T(8,128)(2,1)}) %all-gather.3.cloned.1.call-update) | async-done | bytes 2097168 | tf_op jit(solution)/shard_map/while/body/eval_jaxpr/all_gather | solution.py:80
  464.0 43.4 %all-gather.3.cloned.1.call-done = bf16[1024,1024]{1,0:T(8,128)(2,1)} async-done(((bf16[64,1024]{1,0:T(8,128)(2,1)}), bf16[1024,1024]{1,0:T(8,128)(2,1)}) %all-gather.3.cloned.1.call-update) | async-done | bytes 2097168 | tf_op jit(solution)/shard_map/while/body/eval_jaxpr/all_gather | solution.py:80
  552.3 43.4 %all-gather.3.cloned.1.call-done = bf16[1024,1024]{1,0:T(8,128)(2,1)} async-done(((bf16[64,1024]{1,0:T(8,128)(2,1)}), bf16[1024,1024]{1,0:T(8,128)(2,1)}) %all-gather.3.cloned.1.call-update) | async-done | bytes 2097168 | tf_op jit(solution)/shard_map/while/body/eval_jaxpr/all_gather | solution.py:80
  640.6 43.4 %all-gather.3.cloned.1.call-done = bf16[1024,1024]{1,0:T(8,128)(2,1)} async-done(((bf16[64,1024]{1,0:T(8,128)(2,1)}), bf16[1024,1024]{1,0:T(8,128)(2,1)}) %all-gather.3.cloned.1.call-update) | async-done | bytes 2097168 | tf_op jit(solution)/shard_map/while/body/eval_jaxpr/all_gather | solution.py:80
  722.4 1630.1 %while.53 = (s32[]{:T(128)}, f32[512,1536]{1,0:T(8,128)}, f32[512,512]{1,0:T(8,128)}, f32[512]{0:T(512)}, f32[512]{0:T(512)}, /*index=5*/f32[512,16]{0,1:T(8,128...) while((s32[]{:T(128)}, f32[512,1536]{1,0:T(8,128)}, ...), condition=%wide.region_24.25_spmd.clone.clone, body=%wide.region_9.24_spmd.clone.clone.sunk | while | flops 901157440 | bytes 113356792 | solution.py:262
  797.4 47.7 %reduce-scatter.13.cloned.1.call-done = bf16[64,512]{1,0:T(8,128)(2,1)} async-done(((bf16[1024,512]{1,0:T(8,128)(2,1)}), bf16[64,512]{1,0:T(8,128)(2,1)}) %reduce-scatter.13.cloned.1.call-update) | async-done | bytes 65552 | tf_op jit(solution)/shard_map/while
  846.0 69.3 %reduce-scatter.11.cloned.1.call-done = bf16[64,512]{1,0:T(8,128)(2,1)} async-done(((bf16[1024,512]{1,0:T(8,128)(2,1)}), bf16[64,512]{1,0:T(8,128)(2,1)}) %reduce-scatter.11.cloned.1.call-update) | async-done | bytes 65552 | tf_op jit(solution)/shard_map/while
  1004.0 44.3 %reduce-scatter.13.cloned.1.call-done = bf16[64,512]{1,0:T(8,128)(2,1)} async-done(((bf16[1024,512]{1,0:T(8,128)(2,1)}), bf16[64,512]{1,0:T(8,128)(2,1)}) %reduce-scatter.13.cloned.1.call-update) | async-done | bytes 65552 | tf_op jit(solution)/shard_map/while
  1049.3 69.2 %reduce-scatter.11.cloned.1.call-done = bf16[64,512]{1,0:T(8,128)(2,1)} async-done(((bf16[1024,512]{1,0:T(8,128)(2,1)}), bf16[64,512]{1,0:T(8,128)(2,1)}) %reduce-scatter.11.cloned.1.call-update) | async-done | bytes 65552 | tf_op jit(solution)/shard_map/while
  1208.1 44.3 %reduce-scatter.13.cloned.1.call-done = bf16[64,512]{1,0:T(8,128)(2,1)} async-done(((bf16[1024,512]{1,0:T(8,128)(2,1)}), bf16[64,512]{1,0:T(8,128)(2,1)}) %reduce-scatter.13.cloned.1.call-update) | async-done | bytes 65552 | tf_op jit(solution)/shard_map/while
  1253.4 69.2 %reduce-scatter.11.cloned.1.call-done = bf16[64,512]{1,0:T(8,128)(2,1)} async-done(((bf16[1024,512]{1,0:T(8,128)(2,1)}), bf16[64,512]{1,0:T(8,128)(2,1)}) %reduce-scatter.11.cloned.1.call-update) | async-done | bytes 65552 | tf_op jit(solution)/shard_map/while
  1412.3 44.3 %reduce-scatter.13.cloned.1.call-done = bf16[64,512]{1,0:T(8,128)(2,1)} async-done(((bf16[1024,512]{1,0:T(8,128)(2,1)}), bf16[64,512]{1,0:T(8,128)(2,1)}) %reduce-scatter.13.cloned.1.call-update) | async-done | bytes 65552 | tf_op jit(solution)/shard_map/while
  1457.6 69.2 %reduce-scatter.11.cloned.1.call-done = bf16[64,512]{1,0:T(8,128)(2,1)} async-done(((bf16[1024,512]{1,0:T(8,128)(2,1)}), bf16[64,512]{1,0:T(8,128)(2,1)}) %reduce-scatter.11.cloned.1.call-update) | async-done | bytes 65552 | tf_op jit(solution)/shard_map/while
  1616.7 44.3 %reduce-scatter.13.cloned.1.call-done = bf16[64,512]{1,0:T(8,128)(2,1)} async-done(((bf16[1024,512]{1,0:T(8,128)(2,1)}), bf16[64,512]{1,0:T(8,128)(2,1)}) %reduce-scatter.13.cloned.1.call-update) | async-done | bytes 65552 | tf_op jit(solution)/shard_map/while
  1662.0 69.3 %reduce-scatter.11.cloned.1.call-done = bf16[64,512]{1,0:T(8,128)(2,1)} async-done(((bf16[1024,512]{1,0:T(8,128)(2,1)}), bf16[64,512]{1,0:T(8,128)(2,1)}) %reduce-scatter.11.cloned.1.call-update) | async-done | bytes 65552 | tf_op jit(solution)/shard_map/while
  1821.0 44.3 %reduce-scatter.13.cloned.1.call-done = bf16[64,512]{1,0:T(8,128)(2,1)} async-done(((bf16[1024,512]{1,0:T(8,128)(2,1)}), bf16[64,512]{1,0:T(8,128)(2,1)}) %reduce-scatter.13.cloned.1.call-update) | async-done | bytes 65552 | tf_op jit(solution)/shard_map/while
  1866.3 69.1 %reduce-scatter.11.cloned.1.call-done = bf16[64,512]{1,0:T(8,128)(2,1)} async-done(((bf16[1024,512]{1,0:T(8,128)(2,1)}), bf16[64,512]{1,0:T(8,128)(2,1)}) %reduce-scatter.11.cloned.1.call-update) | async-done | bytes 65552 | tf_op jit(solution)/shard_map/while
  2025.1 44.3 %reduce-scatter.13.cloned.1.call-done = bf16[64,512]{1,0:T(8,128)(2,1)} async-done(((bf16[1024,512]{1,0:T(8,128)(2,1)}), bf16[64,512]{1,0:T(8,128)(2,1)}) %reduce-scatter.13.cloned.1.call-update) | async-done | bytes 65552 | tf_op jit(solution)/shard_map/while
  2070.4 69.4 %reduce-scatter.11.cloned.1.call-done = bf16[64,512]{1,0:T(8,128)(2,1)} async-done(((bf16[1024,512]{1,0:T(8,128)(2,1)}), bf16[64,512]{1,0:T(8,128)(2,1)}) %reduce-scatter.11.cloned.1.call-update) | async-done | bytes 65552 | tf_op jit(solution)/shard_map/while
  2229.5 44.3 %reduce-scatter.13.cloned.1.call-done = bf16[64,512]{1,0:T(8,128)(2,1)} async-done(((bf16[1024,512]{1,0:T(8,128)(2,1)}), bf16[64,512]{1,0:T(8,128)(2,1)}) %reduce-scatter.13.cloned.1.call-update) | async-done | bytes 65552 | tf_op jit(solution)/shard_map/while
  2274.8 69.3 %reduce-scatter.11.cloned.1.call-done = bf16[64,512]{1,0:T(8,128)(2,1)} async-done(((bf16[1024,512]{1,0:T(8,128)(2,1)}), bf16[64,512]{1,0:T(8,128)(2,1)}) %reduce-scatter.11.cloned.1.call-update) | async-done | bytes 65552 | tf_op jit(solution)/shard_map/while
  2359.1 134.2 %all-reduce = (f32[512]{0:T(512)}, f32[512]{0:T(512)}, f32[512,16]{0,1:T(8,128)}) all-reduce(f32[512]{0:T(512)S(1)} %copy-done.36, f32[512]{0:T(512)S(1)} %copy-done.33, f32[512,16]{0,1:T(8,128)S(1)} %copy-done.22), channel_id=1, replica_groups=mesh['dp'=8,'grp'=16] {'dp','grp'}, use_global_device_ids=true, to_apply=%region_27.28 | all-reduce | flops 9216 | bytes 73728 | tf_op jit(solution)/shard_map/psum | solution.py:270
  2500.3 123.2 %all-reduce.6.cloned.1.call-done = (f32[512,1536]{1,0:T(8,128)}, f32[512,512]{1,0:T(8,128)}) async-done(((f32[512,1536]{1,0:T(8,128)}, f32[512,512]{1,0:T(8,128)}), (f32[512,1536]{1,0:T(8,128)}, f32[512,512]{1,0:T(8,128)})) %all-reduce.6.cloned.1.call-update) | async-done | bytes 4194320 | tf_op jit(solution)/shard_map/psum | solution.py:270
  (1611 shorter events, 1265.1 us)
Async XLA Ops:
  9.3 56.7 %all-gather.3.cloned.1.call-start = ((), (), s32[]{:S(2)}) async-start(), calls=%async_computation.8 | async-start | bytes 2228224 | tf_op jit(solution)/shard_map/while/body/eval_jaxpr/all_gather | solution.py:80
  751.7 93.3 %reduce-scatter.13.cloned.1.call-start = ((), (), s32[]{:S(2)}) async-start(), calls=%async_computation.11 | async-start | bytes 1114112 | tf_op jit(solution)/shard_map/while
  781.3 134.0 %reduce-scatter.11.cloned.1.call-start = ((), (), s32[]{:S(2)}) async-start(), calls=%async_computation.10 | async-start | bytes 1114112 | tf_op jit(solution)/shard_map/while
  922.8 52.2 %all-gather.5.cloned.1.call-start = ((), (), s32[]{:S(2)}) async-start(), calls=%async_computation.9 | async-start | bytes 2228224 | tf_op jit(solution)/shard_map/while/body/eval_jaxpr/all_gather | solution.py:199
  955.4 92.9 %reduce-scatter.13.cloned.1.call-start = ((), (), s32[]{:S(2)}) async-start(), calls=%async_computation.11 | async-start | bytes 1114112 | tf_op jit(solution)/shard_map/while
  984.6 133.9 %reduce-scatter.11.cloned.1.call-start = ((), (), s32[]{:S(2)}) async-start(), calls=%async_computation.10 | async-start | bytes 1114112 | tf_op jit(solution)/shard_map/while
  1159.6 92.9 %reduce-scatter.13.cloned.1.call-start = ((), (), s32[]{:S(2)}) async-start(), calls=%async_computation.11 | async-start | bytes 1114112 | tf_op jit(solution)/shard_map/while
  1188.8 133.8 %reduce-scatter.11.cloned.1.call-start = ((), (), s32[]{:S(2)}) async-start(), calls=%async_computation.10 | async-start | bytes 1114112 | tf_op jit(solution)/shard_map/while
  1331.1 52.2 %all-gather.5.cloned.1.call-start = ((), (), s32[]{:S(2)}) async-start(), calls=%async_computation.9 | async-start | bytes 2228224 | tf_op jit(solution)/shard_map/while/body/eval_jaxpr/all_gather | solution.py:199
  1363.8 92.9 %reduce-scatter.13.cloned.1.call-start = ((), (), s32[]{:S(2)}) async-start(), calls=%async_computation.11 | async-start | bytes 1114112 | tf_op jit(solution)/shard_map/while
  1392.9 133.8 %reduce-scatter.11.cloned.1.call-start = ((), (), s32[]{:S(2)}) async-start(), calls=%async_computation.10 | async-start | bytes 1114112 | tf_op jit(solution)/shard_map/while
  1535.3 52.4 %all-gather.5.cloned.1.call-start = ((), (), s32[]{:S(2)}) async-start(), calls=%async_computation.9 | async-start | bytes 2228224 | tf_op jit(solution)/shard_map/while/body/eval_jaxpr/all_gather | solution.py:199
  1567.9 93.1 %reduce-scatter.13.cloned.1.call-start = ((), (), s32[]{:S(2)}) async-start(), calls=%async_computation.11 | async-start | bytes 1114112 | tf_op jit(solution)/shard_map/while
  1597.3 134.0 %reduce-scatter.11.cloned.1.call-start = ((), (), s32[]{:S(2)}) async-start(), calls=%async_computation.10 | async-start | bytes 1114112 | tf_op jit(solution)/shard_map/while
  1772.5 92.9 %reduce-scatter.13.cloned.1.call-start = ((), (), s32[]{:S(2)}) async-start(), calls=%async_computation.11 | async-start | bytes 1114112 | tf_op jit(solution)/shard_map/while
  1801.6 133.8 %reduce-scatter.11.cloned.1.call-start = ((), (), s32[]{:S(2)}) async-start(), calls=%async_computation.10 | async-start | bytes 1114112 | tf_op jit(solution)/shard_map/while
  1943.9 52.2 %all-gather.5.cloned.1.call-start = ((), (), s32[]{:S(2)}) async-start(), calls=%async_computation.9 | async-start | bytes 2228224 | tf_op jit(solution)/shard_map/while/body/eval_jaxpr/all_gather | solution.py:199
  1976.6 92.9 %reduce-scatter.13.cloned.1.call-start = ((), (), s32[]{:S(2)}) async-start(), calls=%async_computation.11 | async-start | bytes 1114112 | tf_op jit(solution)/shard_map/while
  2005.7 134.0 %reduce-scatter.11.cloned.1.call-start = ((), (), s32[]{:S(2)}) async-start(), calls=%async_computation.10 | async-start | bytes 1114112 | tf_op jit(solution)/shard_map/while
  2148.3 52.2 %all-gather.5.cloned.1.call-start = ((), (), s32[]{:S(2)}) async-start(), calls=%async_computation.9 | async-start | bytes 2228224 | tf_op jit(solution)/shard_map/while/body/eval_jaxpr/all_gather | solution.py:199
  2180.9 92.9 %reduce-scatter.13.cloned.1.call-start = ((), (), s32[]{:S(2)}) async-start(), calls=%async_computation.11 | async-start | bytes 1114112 | tf_op jit(solution)/shard_map/while
  2210.1 133.9 %reduce-scatter.11.cloned.1.call-start = ((), (), s32[]{:S(2)}) async-start(), calls=%async_computation.10 | async-start | bytes 1114112 | tf_op jit(solution)/shard_map/while
  2352.6 140.7 %all-reduce.8.cloned.1.call-start = ((), (), s32[]{:S(2)}) async-start(), calls=%async_computation.7 | async-start | bytes 8388608 | tf_op jit(solution)/shard_map/psum | solution.py:267
  2358.3 265.3 %all-reduce.6.cloned.1.call-start = ((), (), s32[]{:S(2)}) async-start(), calls=%async_computation.6 | async-start | bytes 8388608 | tf_op jit(solution)/shard_map/psum | solution.py:270
  (304 other events, 4276.4 us)
Sparse Core Ops, SparseCore 0:
  14.7 51.2 all-gather.2
  781.4 63.5 reduce-scatter.12
  849.3 65.9 reduce-scatter.10
  925.7 49.1 all-gather.4
  984.7 63.5 reduce-scatter.12
  1052.4 66.0 reduce-scatter.10
  1130.0 49.1 all-gather.4
  1188.9 63.5 reduce-scatter.12
  1256.6 65.9 reduce-scatter.10
  1334.1 49.1 all-gather.4
  1393.1 63.5 reduce-scatter.12
  1460.7 65.9 reduce-scatter.10
  1538.6 49.0 all-gather.4
  1597.4 63.5 reduce-scatter.12
  1665.3 65.9 reduce-scatter.10
  1742.8 49.1 all-gather.4
  1801.7 63.5 reduce-scatter.12
  1869.4 65.9 reduce-scatter.10
  1946.9 49.1 all-gather.4
  2005.9 63.5 reduce-scatter.12
  2073.7 66.0 reduce-scatter.10
  2151.3 49.1 all-gather.4
  2210.2 63.5 reduce-scatter.12
  2278.0 65.9 reduce-scatter.10
  (8 shorter events, 364.3 us)
Sparse Core Ops, SparseCore 1:
  2358.3 106.6 all-reduce.7
  2470.6 152.9 all-reduce.5
where the time goes:
time: 2650 us; the launch traced here: 2640 us
  waiting for transfers between devices  1620 us (61%)
  matrix products  326 us (12%)
  local copies, waits for them, and re-layouts  241 us (9%)
  starting transfers between devices  153 us (6%)
  other arithmetic  136 us (5%)
  blocking collectives  134 us (5%)
    while x48, waiting for transfers between devices  912 us
    all_gather x8, waiting for transfers between devices, forward_step(): lax.all_gather(projected[:, model_width:], 'grp', axis=0, tiled=True)  353 us
    psum x1, blocking collectives, on_device(): lax.psum((acc_qkv, acc_out, acc_gain_attn, acc_gain_mix, acc_ctrl), ('dp'...  134 us
    psum x1, waiting for transfers between devices, on_device(): lax.psum((acc_qkv, acc_out, acc_gain_attn, acc_gain_mix, acc_ctrl), ('dp'...  123 us
    while x576, local copies, waits for them, and re-layouts  83.1 us
    all_gather x8, waiting for transfers between devices, backward_step(): lax.all_gather(projected[:, model_width:], 'grp', axis=0, tiled=True)  65.4 us
    all_to_all x8, waiting for transfers between devices, forward_step(): lax.all_to_all(expert_out, 'grp', split_axis=0, concat_axis=1, tiled=True)  54.2 us
    all_to_all x8, starting transfers between devices, backward_step(): lax.all_to_all(grad_expert, 'grp', split_axis=1, concat_axis=0, tiled=True)  53.2 us
  transfers between devices with their start and end apart: 66, of which 65 were waited for; matrix products, arithmetic and copies ran while one was open for 14% of the time, Pallas kernels for 0%

commit v1 on v0

v1 whole, which is shorter than its diff:
```python
import functools

import jax
import jax.numpy as jnp
from jax import lax
from jax.experimental import pallas as pl
from jax.experimental.pallas import tpu as pltpu
from jax.sharding import PartitionSpec as P

HEADS = 8
HEAD_DIM = 64
GROUP = 32
BLOCK = 64
EPSILON = 1e-05
MASKED = -1e30
MESH = pl.DeviceIdType.MESH
F32 = jnp.float32
BF16 = jnp.bfloat16
SEMS = 176


def mm(a, b):
    return lax.dot_general(a, b, (((1,), (0,)), ((), ())), preferred_element_type=F32)


def mm_nt(a, b):
    return lax.dot_general(a, b, (((1,), (1,)), ((), ())), preferred_element_type=F32)


def mm_tn(a, b):
    return lax.dot_general(a, b, (((0,), (0,)), ((), ())), preferred_element_type=F32)


def unit_norm(x):
    centred = x - jnp.mean(x, axis=-1, keepdims=True)
    inv_std = lax.rsqrt(jnp.mean(centred * centred, axis=-1, keepdims=True) + EPSILON)
    return centred * inv_std, inv_std


def norm_back(up, unit, inv_std, gain):
    u = up * gain
    return inv_std * (
        u - jnp.mean(u, axis=-1, keepdims=True) - unit * jnp.mean(u * unit, axis=-1, keepdims=True)
    )


def block_kernel(
    ng, ndp, nx,
    tokens, cotangent, w_qkv, w_out, gain_attn, gain_mix, w_ctrl, w_in, w_back, prefix, group_ids,
    tokens_out, token_grad, reduced, small_out, grad_in, grad_back,
    send_sem, recv_sem, local_sem,
    x_full, cot, ids_send, ids_own, wq, wk, wv, wo, win, wback,
    attn_in, qs, ks, vs, probs, bias, linv, attn, attn_other, resid, mix_in, wc, weights, coef,
    rows_send, rows_all, back_send, back_recv, out_send, mixgrad, gresid, gbranch, gheads,
    acc_k, acc_v, act_q, act_k, act_v, part_send, part_recv, tgrad_send, pay, rs1, red1, rs2, red2, ag1,
    small_pay, small_rs1, small_sib, small_dp, small_fin, acc_b, acc_i,
):
    d, g = lax.axis_index("dp"), lax.axis_index("grp")
    nc, ny = ng // 2, ndp // nx
    c, p = g // 2, g % 2
    sib = g + 1 - 2 * p
    oth = 1 - p
    width = x_full.shape[3]
    half = width // 2
    length = ng * BLOCK
    own = nc * BLOCK
    ff = win.shape[1]
    q_rows = min(256, length // 2)
    n_q = length // q_rows
    per_q = q_rows // (2 * BLOCK)
    cols = ng * 2 * nc

    started, used = [], [0, 0]

    def number():
        used[0] += 1
        return used[0] - 1

    def send(n, src, dst, **device):
        copy = pltpu.make_async_remote_copy(
            src_ref=src, dst_ref=dst, send_sem=send_sem.at[n], recv_sem=recv_sem.at[n],
            device_id=device, device_id_type=MESH,
        )
        copy.start()
        started.append(copy)

    def arrived(n, dst):
        pltpu.make_async_remote_copy(
            src_ref=dst, dst_ref=dst, send_sem=send_sem.at[n], recv_sem=recv_sem.at[n],
            device_id={"grp": sib}, device_id_type=MESH,
        ).wait_recv()

    def local(src, dst):
        copy = pltpu.make_async_copy(src, dst, local_sem.at[used[1]])
        used[1] += 1
        copy.start()
        return copy

    def chip_at(k):
        return lax.rem(c + k, nc)

    def chip_from(k):
        return lax.rem(c + nc - k, nc)

    load_tokens = local(tokens.at[c], x_full.at[c, p])
    loads_qkv = [
        local(w_qkv.at[:, pl.ds(pl.multiple_of(part * width + p * half, 128), half)], dst)
        for part, dst in enumerate((wq, wk, wv))
    ]
    load_out = local(w_out, wo)
    load_cot = local(cotangent.at[c], cot.at[c])
    load_in = local(w_in.at[0], win)
    load_back = local(w_back.at[0], wback)
    barrier = pltpu.get_barrier_semaphore()
    for k in range(1, ng):
        pl.semaphore_signal(barrier, inc=1, device_id={"grp": lax.rem(g + k, ng)}, device_id_type=MESH)
    for k in range(1, ndp):
        pl.semaphore_signal(barrier, inc=1, device_id={"dp": lax.rem(d + k, ndp)}, device_id_type=MESH)
    for b in range(nc):
        ids_send[b] = jnp.zeros((8, 128), jnp.int32)
        ids_send[b, :, 0:BLOCK] = jnp.broadcast_to(group_ids[b : b + 1, :], (8, BLOCK))
    pl.semaphore_wait(barrier, ng + ndp - 2)

    n_tok = [number() for _ in range(nc)]
    n_fwd = [number() for _ in range(nc)]
    n_cot = [number() for _ in range(nc)]
    n_ids = [number() for _ in range(nc)]
    for k in range(1, nc):
        to = chip_at(k)
        send(n_tok[k], tokens.at[to], x_full.at[c, p], grp=to * 2 + p)
    for k in range(1, nc):
        to = chip_at(k)
        send(n_ids[k], ids_send.at[to], ids_own.at[c], grp=to * 2 + p)
    for k in range(1, nc):
        to = chip_at(k)
        send(n_cot[k], cotangent.at[to], cot.at[c], grp=to * 2 + p)
    ids_own[c] = ids_send[c]
    load_tokens.wait()
    send(n_fwd[0], x_full.at[c, p], x_full.at[c, p], grp=sib)

    prefix_len = prefix[c]
    hl = length // 2

    def mask_rows(b, carry):
        row = lax.broadcasted_iota(jnp.int32, (BLOCK, hl), 0) + b * BLOCK
        col = lax.broadcasted_iota(jnp.int32, (BLOCK, hl), 1)
        bias[pl.ds(pl.multiple_of(b * BLOCK, BLOCK), BLOCK), :] = jnp.where(
            (col <= row) | (col < prefix_len), 0.0, MASKED
        )
        return carry

    lax.fori_loop(0, hl // BLOCK, mask_rows, 0)
    spread = (
        lax.broadcasted_iota(jnp.int32, (ng, cols), 1) // (2 * nc)
        == lax.broadcasted_iota(jnp.int32, (ng, cols), 0)
    ).astype(F32)
    wc[...] = mm(w_ctrl[...].astype(F32), spread).astype(BF16)

    for k in range(1, nc):
        block = x_full.at[chip_from(k), p]
        arrived(n_tok[k], block)
        send(n_fwd[k], block, block, grp=sib)
    for load in loads_qkv:
        load.wait()

    gain_a = gain_attn[...]
    gain_m = gain_mix[...]

    def project(par):
        def rows(b, carry):
            unit, _ = unit_norm(x_full[b, par].astype(F32))
            attn_in[b, par] = (unit * gain_a).astype(BF16)
            return carry

        lax.fori_loop(0, nc, rows, 0)
        a = attn_in[:, par].reshape(own, width)
        qs[:, par] = (mm(a, wq[...]).astype(BF16) * BF16(HEAD_DIM**-0.5)).reshape(nc, BLOCK, half)
        ks[:, par] = mm(a, wk[...]).astype(BF16).reshape(nc, BLOCK, half)
        vs[:, par] = mm(a, wv[...]).astype(BF16).reshape(nc, BLOCK, half)

    project(p)
    for k in range(nc):
        arrived(n_fwd[k], x_full.at[chip_from(k), oth])
    project(oth)

    lane = lax.broadcasted_iota(jnp.int32, (1, 128), 1)
    low_lane = lane < HEAD_DIM
    keep_f = [jnp.where(low_lane, 1.0, 0.0), jnp.where(low_lane, 0.0, 1.0)]
    keep = [m.astype(BF16) for m in keep_f]
    causal = jnp.where(
        lax.broadcasted_iota(jnp.int32, (q_rows, q_rows), 1)
        <= lax.broadcasted_iota(jnp.int32, (q_rows, q_rows), 0),
        0.0,
        MASKED,
    )

    def key_range(i):
        return max(length // 2, (i + 1) * q_rows)

    def rows_of(ref, i, n, pair):
        return ref[i : i + n, :, :, pair * 128 : pair * 128 + 128].reshape(n * 2 * BLOCK, 128)

    n_mix = number()
    for i in range(n_q):
        extent = key_range(i)
        blocks = extent // (2 * BLOCK)
        for pair in range(2):
            q = rows_of(qs, i * per_q, per_q, pair)
            k_ = rows_of(ks, 0, blocks, pair)
            v_ = rows_of(vs, 0, blocks, pair)
            outs, invs = [], []
            for h in range(2):
                s = mm_nt(q * keep[h], k_)
                if (i + 1) * q_rows <= hl:
                    parts = [s + bias[i * q_rows : (i + 1) * q_rows, :]]
                else:
                    parts = [s[:, : extent - q_rows], s[:, extent - q_rows :] + causal]
                top = functools.reduce(
                    jnp.maximum, [jnp.max(part, axis=-1, keepdims=True) for part in parts]
                )
                at = 0
                for part in parts:
                    probs[pair * 2 + h, i * q_rows : (i + 1) * q_rows, at : at + part.shape[1]] = jnp.exp(part - top).astype(BF16)
                    at += part.shape[1]
                o = mm(
                    probs[pair * 2 + h, i * q_rows : (i + 1) * q_rows, :extent],
                    v_ * keep[h] + keep[1 - h],
                )
                inv = 1.0 / pltpu.roll(o, HEAD_DIM, 1)
                outs.append(o * inv)
                invs.append(inv)
            shape = (per_q, 2, BLOCK, 128)
            at = slice(pair * 128, pair * 128 + 128)
            attn[i * per_q : (i + 1) * per_q, :, :, at] = (
                jnp.where(low_lane, outs[0], outs[1]).astype(BF16).reshape(shape)
            )
            linv[i * per_q : (i + 1) * per_q, :, :, at] = jnp.where(
                low_lane, invs[0], invs[1]
            ).reshape(shape)
    send(n_mix, attn.at[:, oth], attn_other, grp=sib)
    load_out.wait()
    for k in range(1, nc):
        arrived(n_cot[k], cot.at[chip_from(k)])
        arrived(n_ids[k], ids_own.at[chip_from(k)])
    load_cot.wait()
    mixed_own = mm(attn[:, p].reshape(own, half), wo[p])
    arrived(n_mix, attn_other)
    resid[...] = (
        x_full[:, p].reshape(own, width).astype(F32)
        + mixed_own
        + mm(attn_other[...].reshape(own, half), wo[oth])
    )

    def block_rows(b):
        return pl.ds(pl.multiple_of(b * BLOCK, BLOCK), BLOCK)

    def mix_rows(b, carry):
        unit, _ = unit_norm(resid[block_rows(b), :])
        mix_in[block_rows(b), :] = (unit * gain_m).astype(BF16)
        return carry

    lax.fori_loop(0, nc, mix_rows, 0)
    weights[...] = mm(mix_in[...], wc[...])
    place = lax.broadcasted_iota(jnp.int32, (1, cols), 1) % (2 * nc)
    diagonal = lax.broadcasted_iota(jnp.int32, (BLOCK, 128), 0) == lax.broadcasted_iota(
        jnp.int32, (BLOCK, 128), 1
    )

    def member_rows(b, carry):
        ids = jnp.broadcast_to(ids_own[b, 0:1, :].astype(F32), (BLOCK, 128))
        id_col = jnp.sum(jnp.where(diagonal, ids, 0.0), axis=1, keepdims=True)
        member = (place - 2 * b).astype(F32) == id_col
        weights[block_rows(b), :] = jnp.where(member, weights[block_rows(b), :], MASKED)
        return carry

    lax.fori_loop(0, nc, member_rows, 0)
    top = jnp.max(weights[...], axis=0, keepdims=True)
    exponent = jnp.exp(weights[...] - top)
    w256 = exponent / jnp.sum(exponent, axis=0, keepdims=True)
    weights[...] = w256
    coef[...] = w256.astype(BF16)
    rows_send[0] = mm_tn(coef[...], mix_in[...]).astype(BF16).reshape(ng, 2 * nc, width)
    cot_rows = cot[...].reshape(own, width)
    rows_send[1] = mm_tn(coef[...], cot_rows).astype(BF16).reshape(ng, 2 * nc, width)

    n_rows = [number() for _ in range(ng)]
    for k in range(1, ng):
        to = lax.rem(g + k, ng)
        send(n_rows[k], rows_send.at[:, to], rows_all.at[d, :, g], grp=to)
    rows_all[d, :, g] = rows_send[:, g]
    load_in.wait()
    load_back.wait()
    for k in range(1, ng):
        arrived(n_rows[k], rows_all.at[d, :, lax.rem(g + ng - k, ng)])

    dx, dy = d // ny, d % ny
    n_m = [[number() for _ in range(ny)] for _ in range(nx)]
    n_g = [[number() for _ in range(ny)] for _ in range(nx)]
    x_to = (1 - dx) * ny + dy if nx == 2 else d

    def y_at(k, x):
        return x * ny + lax.rem(dy + k, ny)

    def y_from(k, x):
        return x * ny + lax.rem(dy + ny - k, ny)

    if nx == 2:
        send(n_m[1][0], rows_all.at[d, 0], rows_all.at[d, 0], dp=x_to)
    for k in range(1, ny):
        send(n_g[0][k], rows_all.at[d, 1], rows_all.at[d, 1], dp=y_at(k, dx))
        send(n_m[0][k], rows_all.at[d, 0], rows_all.at[d, 0], dp=y_at(k, dx))
    if nx == 2:
        send(n_g[1][0], rows_all.at[d, 1], rows_all.at[d, 1], dp=x_to)

    mixed = rows_all[d, 0].reshape(cols, width)
    gexp = rows_all[d, 1].reshape(cols, width)
    tile = min(512, ff)

    def expert_tile(f, mixed, gexp):
        at = pl.ds(pl.multiple_of(f * tile, tile), tile)
        w1, w2 = win[:, at], wback[at, :]
        pre = mm(mixed, w1)
        sig = jax.nn.sigmoid(pre)
        hidden = (pre * sig).astype(BF16)
        ghid = mm_nt(gexp, w2)
        gpre = (ghid * (sig * (1.0 + pre * (1.0 - sig)))).astype(BF16)
        return hidden, gpre, w1, w2

    e_out = g_mixed = None
    for f in range(ff // tile):
        hidden, gpre, w1, w2 = expert_tile(f, mixed, gexp)
        e_part, g_part = mm(hidden, w2), mm_nt(gpre, w1)
        e_out = e_part if e_out is None else e_out + e_part
        g_mixed = g_part if g_mixed is None else g_mixed + g_part
    back_send[0] = e_out.astype(BF16).reshape(ng, 2 * nc, width)
    back_send[1] = g_mixed.astype(BF16).reshape(ng, 2 * nc, width)
    n_back = [number() for _ in range(ng)]
    for k in range(1, ng):
        to = lax.rem(g + k, ng)
        send(n_back[k], back_send.at[:, to], back_recv.at[:, g], grp=to)
    back_recv[:, g] = back_send[:, g]

    if nx == 2:
        from_x = rows_all.at[x_to, 0]
        arrived(n_m[1][0], from_x)
        for k in range(1, ny):
            send(n_m[1][k], from_x, from_x, dp=y_at(k, dx))
    for k in range(1, ng):
        arrived(n_back[k], back_recv.at[:, lax.rem(g + ng - k, ng)])

    e_rows = back_recv[0].reshape(cols, width)
    g_rows = back_recv[1].reshape(cols, width)
    out_send[...] = (resid[...] + mm(coef[...], e_rows)).astype(BF16).reshape(nc, BLOCK, width)
    n_out = [number() for _ in range(nc)]
    for k in range(1, nc):
        to = chip_at(k)
        send(n_out[k], out_send.at[to], tokens_out.at[c], grp=to * 2 + p)
    keep_out = local(out_send.at[c], tokens_out.at[c])
    dots = mm_nt(cot_rows, e_rows) + mm_nt(mix_in[...], g_rows)
    w256 = weights[...]
    inner = jnp.sum(w256 * dots, axis=0, keepdims=True)
    glogit = (w256 * (dots - inner)).astype(BF16)
    mixgrad[...] = mm(coef[...], g_rows) + mm_nt(glogit, wc[...])
    ctrl = mm_tn(glogit, mix_in[...]).reshape(ng, 2 * nc, width).sum(axis=1)

    def resid_rows(b, total):
        unit, inv_std = unit_norm(resid[block_rows(b), :])
        up = mixgrad[block_rows(b), :]
        grad = cot[b].astype(F32) + norm_back(up, unit, inv_std, gain_m)
        gresid[block_rows(b), :] = grad
        gbranch[p, b] = grad.astype(BF16)
        return total + jnp.sum(up * unit, axis=0, keepdims=True)

    gain_m_part = lax.fori_loop(0, nc, resid_rows, jnp.zeros((1, width), F32))
    n_branch = number()
    send(n_branch, gbranch.at[p], gbranch.at[p], grp=sib)

    def head_grads(par):
        raw = mm_nt(gbranch[par].reshape(own, width), wo[p])
        scaled = (raw * linv[:, par].reshape(own, half)).astype(BF16)
        prod = scaled.astype(F32) * attn[:, par].reshape(own, half).astype(F32)
        for pair in range(2):
            at = slice(pair * 128, pair * 128 + 128)
            for h in range(2):
                delta = jnp.sum(prod[:, at] * keep_f[h], axis=1, keepdims=True)
                high = delta.astype(BF16).astype(F32)
                low = delta - high
                first = HEAD_DIM * (1 - h)
                extra = jnp.where(lane == first, -high, jnp.where(lane == first + 1, -low, 0.0))
                gheads[pair * 2 + h, :, par] = (
                    scaled[:, at] * keep[h] + extra.astype(BF16)
                ).reshape(nc, BLOCK, 128)

    head_grads(p)
    arrived(n_branch, gbranch.at[oth])
    head_grads(oth)

    if nx == 2:
        arrived(n_g[1][0], rows_all.at[x_to, 1])
        for k in range(1, ny):
            block = rows_all.at[y_from(k, dx), 1]
            arrived(n_g[0][k], block)
            send(n_g[1][k], block, block, dp=x_to)
    else:
        for k in range(1, ny):
            arrived(n_g[0][k], rows_all.at[y_from(k, dx), 1])

    acc_k[...] = jnp.zeros_like(acc_k)
    acc_v[...] = jnp.zeros_like(acc_v)
    for i in range(n_q):
        extent = key_range(i)
        blocks = extent // (2 * BLOCK)
        span = slice(i * q_rows, (i + 1) * q_rows)
        for pair in range(2):
            at = slice(pair * 128, pair * 128 + 128)
            q = rows_of(qs, i * per_q, per_q, pair)
            k_ = rows_of(ks, 0, blocks, pair)
            v_ = rows_of(vs, 0, blocks, pair)
            grads, dqs = [], []
            for h in range(2):
                up = gheads[pair * 2 + h, i * per_q : (i + 1) * per_q].reshape(q_rows, 128)
                dp = mm_nt(up, v_ * keep[h] + keep[1 - h]).astype(BF16)
                ds = probs[pair * 2 + h, span, :extent] * dp
                grads.append(up * keep[h])
                dqs.append(mm(ds, k_))
                part_k = mm_tn(ds, q * keep[h])
                part_v = mm_tn(probs[pair * 2 + h, span, :extent], grads[h])
                acc_k[:extent, at] += part_k
                acc_v[:extent, at] += part_v
            act_q[i * per_q : (i + 1) * per_q, :, :, at] = (
                (jnp.where(low_lane, dqs[0], dqs[1]) * HEAD_DIM**-0.5)
                .astype(BF16)
                .reshape(per_q, 2, BLOCK, 128)
            )
    act_k[...] = acc_k[...].astype(BF16).reshape(nc, 2, BLOCK, half)
    act_v[...] = acc_v[...].astype(BF16).reshape(nc, 2, BLOCK, half)

    def act_grad(par):
        return sum(
            mm_nt(act[:, par].reshape(own, half), w[...])
            for act, w in ((act_q, wq), (act_k, wk), (act_v, wv))
        )

    part_send[...] = act_grad(oth).astype(BF16).reshape(nc, BLOCK, width)
    n_part = number()
    send(n_part, part_send, part_recv, grp=sib)
    mixgrad[...] = act_grad(p)

    a = attn_in[...].reshape(length, width)
    for part, act in enumerate((act_q, act_k, act_v)):
        grad = mm_tn(a, act[...].reshape(length, half)).astype(BF16)
        pay[part * half : (part + 1) * half, :half] = grad[:half]
        pay[part * half : (part + 1) * half, half:] = grad[half:]
    pay[3 * half : 4 * half, :] = sum(
        mm_tn(attn[:, par].reshape(own, half), gbranch[par].reshape(own, width)) for par in range(2)
    ).astype(BF16)
    ra = 4 * half // nc
    rb = ra // ndp
    n_rs1 = [number() for _ in range(nc)]
    for k in range(1, nc):
        to = chip_at(k)
        send(n_rs1[k], pay.at[pl.ds(pl.multiple_of(to * ra, ra), ra)], rs1.at[c], grp=to * 2 + p)

    arrived(n_part, part_recv)

    def grad_rows(b, total):
        unit, inv_std = unit_norm(x_full[b, p].astype(F32))
        up = mixgrad[block_rows(b), :] + part_recv[b].astype(F32)
        grad = gresid[block_rows(b), :] + norm_back(up, unit, inv_std, gain_a)
        tgrad_send[b] = grad.astype(BF16)
        return total + jnp.sum(up * unit, axis=0, keepdims=True)

    gain_a_part = lax.fori_loop(0, nc, grad_rows, jnp.zeros((1, width), F32))
    n_tg = [number() for _ in range(nc)]
    for k in range(1, nc):
        to = chip_at(k)
        send(n_tg[k], tgrad_send.at[to], token_grad.at[c], grp=to * 2 + p)
    keep_tg = local(tgrad_send.at[c], token_grad.at[c])

    tiles = 8 // nc
    for j in range(8):
        r, l = j // 4, j % 4
        if ng >= 8 * (r + 1):
            small_pay[j // tiles, j % tiles] = ctrl[r * 8 : r * 8 + 8, l * 128 : l * 128 + 128]
        else:
            small_pay[j // tiles, j % tiles] = jnp.zeros((8, 128), F32)
            if ng > 8 * r:
                small_pay[j // tiles, j % tiles, : ng - 8 * r] = ctrl[r * 8 : ng, l * 128 : l * 128 + 128]
    for j in range(nc):
        for l in range(4):
            small_pay[j, tiles, l : l + 1] = gain_a_part[:, l * 128 : l * 128 + 128]
            small_pay[j, tiles, 4 + l : 5 + l] = gain_m_part[:, l * 128 : l * 128 + 128]
    n_s1 = [number() for _ in range(nc)]
    for k in range(1, nc):
        to = chip_at(k)
        send(n_s1[k], small_pay.at[to], small_rs1.at[c], grp=to * 2 + p)
    small_rs1[c] = small_pay[c]
    rs1[c] = pay[pl.ds(pl.multiple_of(c * ra, ra), ra), :]

    for k in range(1, nc):
        arrived(n_rs1[k], rs1.at[chip_from(k)])
    total = rs1[0].astype(F32)
    for j in range(1, nc):
        total = total + rs1[j].astype(F32)
    red1[...] = total.astype(BF16)
    n_rs2 = [number() for _ in range(ndp)]
    for k in range(1, ndp):
        to = lax.rem(d + k, ndp)
        send(n_rs2[k], red1.at[pl.ds(pl.multiple_of(to * rb, rb), rb)], rs2.at[d], dp=to)
    rs2[d] = red1[pl.ds(pl.multiple_of(d * rb, rb), rb), :]
    for k in range(1, nc):
        arrived(n_s1[k], small_rs1.at[chip_from(k)])
    small_sib[p] = small_rs1[...].sum(axis=0)
    n_ss = number()
    send(n_ss, small_sib.at[p], small_sib.at[p], grp=sib)

    if nx == 2:
        for k in range(1, ny):
            arrived(n_g[1][k], rows_all.at[y_from(k, 1 - dx), 1])
            arrived(n_m[1][k], rows_all.at[y_from(k, 1 - dx), 0])
    for k in range(1, ny):
        arrived(n_m[0][k], rows_all.at[y_from(k, dx), 0])

    for k in range(1, ndp):
        arrived(n_rs2[k], rs2.at[lax.rem(d + ndp - k, ndp)])
    total = rs2[0].astype(F32)
    for j in range(1, ndp):
        total = total + rs2[j].astype(F32)
    red2[...] = total.astype(BF16)
    n_ag1 = [number() for _ in range(ndp)]
    mine = ag1.at[pl.ds(pl.multiple_of(d * rb, rb), rb)]
    for k in range(1, ndp):
        send(n_ag1[k], red2, mine, dp=lax.rem(d + k, ndp))
    ag1[pl.ds(pl.multiple_of(d * rb, rb), rb), :] = red2[...]
    arrived(n_ss, small_sib.at[oth])
    small_dp[d] = small_sib[0] + small_sib[1]
    n_sd = [number() for _ in range(ndp)]
    for k in range(1, ndp):
        send(n_sd[k], small_dp.at[d], small_dp.at[d], dp=lax.rem(d + k, ndp))

    step = min(2, ndp)
    n_half = 2
    for f in range(ff // tile):
        if f == 1:
            for k in range(1, ndp):
                frm = lax.rem(d + ndp - k, ndp)
                arrived(n_ag1[k], ag1.at[pl.ds(pl.multiple_of(frm * rb, rb), rb)])
            n_ag2 = [number() for _ in range(nc)]
            n_ag3 = [number() for _ in range(nc)]
            place_c = reduced.at[p, pl.ds(pl.multiple_of(c * ra, ra), ra)]
            for k in range(1, nc):
                send(n_ag2[k], ag1, place_c, grp=chip_at(k) * 2 + p)
            send(n_ag3[0], ag1, place_c, grp=sib)
            keep_red = local(ag1, place_c)
            for k in range(1, ndp):
                arrived(n_sd[k], small_dp.at[lax.rem(d + ndp - k, ndp)])
            small_fin[...] = small_dp[...].sum(axis=0)
            n_sg = [number() for _ in range(nc)]
            for k in range(1, nc):
                send(n_sg[k], small_fin, small_out.at[c], grp=chip_at(k) * 2 + p)
            keep_small = local(small_fin, small_out.at[c])
        if f == ff // tile - 1:
            for k in range(1, nc):
                place_k = reduced.at[p, pl.ds(pl.multiple_of(chip_from(k) * ra, ra), ra)]
                arrived(n_ag2[k], place_k)
                send(n_ag3[k], place_k, place_k, grp=sib)
        slot = f % n_half

        def chunk(j, carry, f=f, slot=slot):
            m_rows = rows_all[pl.ds(j * step, step), 0].reshape(step * cols, width)
            g_rows = rows_all[pl.ds(j * step, step), 1].reshape(step * cols, width)
            hidden, gpre, _, _ = expert_tile(f, m_rows, g_rows)
            part_b, part_i = mm_tn(hidden, g_rows), mm_tn(m_rows, gpre)

            @pl.when(j == 0)
            def _():
                acc_b[slot] = part_b
                acc_i[slot] = part_i

            @pl.when(j > 0)
            def _():
                acc_b[slot] += part_b
                acc_i[slot] += part_i

            return carry

        if f >= n_half:
            stores[f - n_half][0].wait()
            stores[f - n_half][1].wait()
        else:
            stores = [] if f == 0 else stores
        lax.fori_loop(0, ndp // step, chunk, 0)
        stores.append(
            (
                local(acc_b.at[slot], grad_back.at[0, f * tile : (f + 1) * tile, :]),
                local(acc_i.at[slot], grad_in.at[0, :, f * tile : (f + 1) * tile]),
            )
        )

    for b, i in stores[-n_half:]:
        b.wait()
        i.wait()
    for k in range(1, nc):
        arrived(n_out[k], tokens_out.at[chip_from(k)])
        arrived(n_tg[k], token_grad.at[chip_from(k)])
        arrived(n_sg[k], small_out.at[chip_from(k)])
    for k in range(nc):
        arrived(n_ag3[k], reduced.at[oth, pl.ds(pl.multiple_of(chip_from(k) * ra, ra), ra)])
    for copy in (keep_out, keep_tg, keep_red, keep_small):
        copy.wait()
    for copy in started:
        copy.wait_send()


def on_device(
    ng, ndp, nx,
    tokens, cotangent, w_qkv, w_out, gain_attn, gain_mix, w_ctrl, w_in, w_back, prefix, group_ids,
):
    nc = ng // 2
    width = tokens.shape[2]
    half = width // 2
    length, own = ng * BLOCK, nc * BLOCK
    ff = w_in.shape[2]
    cols = ng * 2 * nc
    ra = 4 * half // nc
    tile = min(512, ff)
    tiles = 8 // nc
    vm = pltpu.VMEM
    anywhere = pl.BlockSpec(memory_space=pl.ANY)
    in_vmem = pl.BlockSpec(memory_space=pltpu.VMEM)
    in_smem = pl.BlockSpec(memory_space=pltpu.SMEM)
    scratch = [
        pltpu.SemaphoreType.DMA((SEMS,)),
        pltpu.SemaphoreType.DMA((SEMS,)),
        pltpu.SemaphoreType.DMA((32,)),
        vm((nc, 2, BLOCK, width), BF16),
        vm((nc, BLOCK, width), BF16),
        vm((nc, 8, 128), jnp.int32),
        vm((nc, 8, 128), jnp.int32),
        vm((width, half), BF16),
        vm((width, half), BF16),
        vm((width, half), BF16),
        vm((2, half, width), BF16),
        vm((width, ff), BF16),
        vm((ff, width), BF16),
        vm((nc, 2, BLOCK, width), BF16),
        vm((nc, 2, BLOCK, half), BF16),
        vm((nc, 2, BLOCK, half), BF16),
        vm((nc, 2, BLOCK, half), BF16),
        vm((4, length, length), BF16),
        vm((length // 2, length // 2), F32),
        vm((nc, 2, BLOCK, half), F32),
        vm((nc, 2, BLOCK, half), BF16),
        vm((nc, BLOCK, half), BF16),
        vm((own, width), F32),
        vm((own, width), BF16),
        vm((width, cols), BF16),
        vm((own, cols), F32),
        vm((own, cols), BF16),
        vm((2, ng, 2 * nc, width), BF16),
        vm((ndp, 2, ng, 2 * nc, width), BF16),
        vm((2, ng, 2 * nc, width), BF16),
        vm((2, ng, 2 * nc, width), BF16),
        vm((nc, BLOCK, width), BF16),
        vm((own, width), F32),
        vm((own, width), F32),
        vm((2, nc, BLOCK, width), BF16),
        vm((4, nc, 2, BLOCK, 128), BF16),
        vm((length, half), F32),
        vm((length, half), F32),
        vm((nc, 2, BLOCK, half), BF16),
        vm((nc, 2, BLOCK, half), BF16),
        vm((nc, 2, BLOCK, half), BF16),
        vm((nc, BLOCK, width), BF16),
        vm((nc, BLOCK, width), BF16),
        vm((nc, BLOCK, width), BF16),
        vm((4 * half, width), BF16),
        vm((nc, ra, width), BF16),
        vm((ra, width), BF16),
        vm((ndp, ra // ndp, width), BF16),
        vm((ra // ndp, width), BF16),
        vm((ra, width), BF16),
        vm((nc, tiles + 1, 8, 128), F32),
        vm((nc, tiles + 1, 8, 128), F32),
        vm((2, tiles + 1, 8, 128), F32),
        vm((ndp, tiles + 1, 8, 128), F32),
        vm((tiles + 1, 8, 128), F32),
        vm((2, tile, width), F32),
        vm((2, width, tile), F32),
    ]
    tokens_out, token_grad, reduced, small, grad_in, grad_back = pl.pallas_call(
        functools.partial(block_kernel, ng, ndp, nx),
        out_shape=[
            jax.ShapeDtypeStruct(tokens.shape, BF16),
            jax.ShapeDtypeStruct(tokens.shape, BF16),
            jax.ShapeDtypeStruct((2, 4 * half, width), BF16),
            jax.ShapeDtypeStruct((nc, tiles + 1, 8, 128), F32),
            jax.ShapeDtypeStruct(w_in.shape, F32),
            jax.ShapeDtypeStruct(w_back.shape, F32),
        ],
        in_specs=[anywhere] * 4 + [in_vmem] * 3 + [anywhere] * 2 + [in_smem, in_vmem],
        out_specs=[anywhere] * 6,
        scratch_shapes=scratch,
        compiler_params=pltpu.CompilerParams(
            collective_id=0, has_side_effects=True, vmem_limit_bytes=60 * 1024 * 1024
        ),
        name="of_tokens_block",
    )(
        tokens, cotangent, w_qkv, w_out.reshape(2, half, width), gain_attn.reshape(1, width),
        gain_mix.reshape(1, width), w_ctrl, w_in, w_back, prefix, group_ids,
    )
    halves = reduced.reshape(2, 4, half, 2, half)
    grad_qkv = halves[:, :3].transpose(3, 2, 1, 0, 4).reshape(width, 3 * width).astype(F32)
    grad_out = reduced[:, 3 * half :].reshape(width, width).astype(F32)
    ctrl_tiles = small[:, :tiles].reshape(2, 4, 8, 128).transpose(0, 2, 1, 3).reshape(16, width)
    grad_ctrl = ctrl_tiles[:ng].T
    grad_gain_attn = small[0, tiles, :4].reshape(width)
    grad_gain_mix = small[0, tiles, 4:].reshape(width)
    return (
        tokens_out,
        token_grad.astype(F32),
        grad_qkv,
        grad_out,
        grad_gain_attn,
        grad_gain_mix,
        grad_ctrl,
        grad_in,
        grad_back,
    )


def solution(mesh):
    ng, ndp = mesh.shape["grp"], mesh.shape["dp"]
    in_specs = (
        P("dp", "grp", None),
        P("dp", "grp", None),
        P(),
        P(),
        P(),
        P(),
        P(),
        P("grp", None, None),
        P("grp", None, None),
        P("dp"),
        P("dp", "grp"),
    )
    out_specs = (
        P("dp", "grp", None),
        P("dp", "grp", None),
        P(),
        P(),
        P(),
        P(),
        P(),
        P("grp", None, None),
        P("grp", None, None),
    )
    return jax.shard_map(
        functools.partial(on_device, ng, ndp, 2),
        mesh=mesh, in_specs=in_specs, out_specs=out_specs, check_vma=False,
    )
```

time: 2650 us -> 169 us (0.06)
  waiting for transfers between devices: 1620 us -> 0 us
  matrix products: 326 us -> 0 us
  local copies, waits for them, and re-layouts: 241 us -> 20.9 us
  starting transfers between devices: 153 us -> 0 us
  Pallas kernels: 0 us -> 143 us
  blocking collectives: 134 us -> 0 us
  other arithmetic: 136 us -> 4.36 us
    while x48 -> x0, waiting for transfers between devices: 912 us -> none
    all_gather x16 -> x0, waiting for transfers between devices: 419 us -> none  [the longest x8 353 us: forward_step(): lax.all_gather(projected[:, model_width:], 'grp', axis=0, tiled=True)]
    dot_general x280 -> x0, matrix products: 326 us -> none  [the longest x8 39.6 us: backward_step(): jnp.einsum('gef,ged->efd', hidden, grad_owner, preferred_element_type=jnp...]
    all_to_all x32 -> x0, waiting for transfers between devices: 170 us -> none  [the longest x8 54.2 us: forward_step(): lax.all_to_all(expert_out, 'grp', split_axis=0, concat_axis=1, tiled=True)]
    all_to_all x32 -> x0, starting transfers between devices: 152 us -> none  [the longest x8 53.2 us: backward_step(): lax.all_to_all(grad_expert, 'grp', split_axis=1, concat_axis=0, tiled=True)]
    pallas_call x0 -> x1, Pallas kernels: none -> 143 us  [on_device(): pl.pallas_call(functools.partial(block_kernel, ng, ndp, nx), out_shape=[j...]
    psum x1 -> x0, blocking collectives: 134 us -> none  [on_device(): lax.psum((acc_qkv, acc_out, acc_gain_attn, acc_gain_mix, acc_ctrl), ('dp'...]
    psum x2 -> x0, waiting for transfers between devices: 123 us -> none  [the longest x1 123 us: on_device(): lax.psum((acc_qkv, acc_out, acc_gain_attn, acc_gain_mix, acc_ctrl), ('dp'...]
  transfers between devices with their start and end apart: 66 -> 0, of which waited for: 65 -> 0; matrix products, arithmetic and copies ran while one was open for 14% -> 0% of each run, Pallas kernels for 0% -> 0%
where the time goes in v1:
time: 169 us
  Pallas kernels  143 us (85%)
  local copies, waits for them, and re-layouts  20.9 us (12%)
  other arithmetic  4.36 us (3%)
    pallas_call x1, Pallas kernels, on_device(): pl.pallas_call(functools.partial(block_kernel, ng, ndp, nx), out_shape=[j...  143 us
    unnamed x10, local copies, waits for them, and re-layouts  9.07 us
    convert_element_type x2, local copies, waits for them, and re-layouts, on_device(): halves[:, :3].transpose(3, 2, 1, 0, 4).reshape(width, 3 * width).astype(F32)  6.12 us

profile of v1, /device:TPU:1, one launch (start us, length us, event | category | flops | bytes accessed | tf_op | source)
XLA Modules:
  0.0 168.9 jit_solution(11481835467620241885)
XLA Ops:
  0.6 1.5 copy.20.w_ctrl
  2.1 142.9 %of_tokens_block.1 = (bf16[8,64,512]{2,1,0:T(8,128)(2,1)}, bf16[8,64,512]{2,1,0:T(8,128)(2,1)}, bf16[2,1024,512]{2,1,0:T(8,128)(2,1)}, f32[8,2,8,128]{3,2,1,0:T(...) custom-call(bf16[8,64,512]{2,1,0:T(8,128)(2,1)} %tokens.1, bf16[8,64,512]{2,1,0:T(8,128)(2,1)} %cotangent.1, ...), custom_call_target="tpu_custom_call" | custom-call | tf_op jit(solution)/shard_map/of_tokens_block/pallas_call | solution.py:691
  145.0 1.3 slice_bitcast_fusion
  146.4 2.5 %reshape.45 = bf16[2,4,256,2,256]{4,3,2,1,0:T(2,128)(2,1)S(1)} reshape(bf16[2,1024,512]{2,1,0:T(8,128)(2,1)} %get-tuple-element.17) | data formatting | bytes 4194304 | tf_op jit(solution)/shard_map/reshape | solution.py:712
  148.9 1.1 convert_bitcast_fusion
  150.0 2.4 %copy.21 = f32[2,256,3,2,256]{4,3,2,1,0:T(2,128)S(1)} copy(f32[2,256,3,2,256]{4,0,1,2,3:T(2,128)S(1)} %convert_bitcast_fusion) | data formatting | bytes 6291456 | tf_op jit(solution)/shard_map/convert_element_type | solution.py:713
  152.4 0.0 copy-start.2
  152.4 3.7 %reshape.48 = f32[512,1536]{1,0:T(8,128)} reshape(f32[2,256,3,2,256]{4,3,2,1,0:T(2,128)S(1)} %copy.21) | data formatting | bytes 6291456 | tf_op jit(solution)/shard_map/convert_element_type | solution.py:713
  156.1 0.0 copy-start.1
  156.1 1.2 slice.16
  157.4 1.1 bitcast_convert_fusion
  158.5 0.0 copy-done.2
  158.5 0.6 slice.19
  159.1 2.1 %convert_element_type.18 = f32[8,64,512]{2,1,0:T(8,128)} convert(bf16[8,64,512]{2,1,0:T(8,128)(2,1)} %get-tuple-element.16) | non-fusion elementwise | flops 262144 | bytes 1572864 | tf_op jit(solution)/shard_map/convert_element_type | solution.py:721
  161.3 1.9 %copy.25 = bf16[8,64,512]{2,1,0:T(8,128)(2,1)} copy(bf16[8,64,512]{2,1,0:T(8,128)(2,1)} %get-tuple-element.32) | data formatting | bytes 1048576
  163.1 0.0 copy-done.1
  163.1 0.0 copy-start
  163.1 2.1 %copy.26 = f32[1,512,2048]{2,1,0:T(8,128)} copy(f32[1,512,2048]{2,1,0:T(8,128)S(1)} %copy-done.1) | data formatting | bytes 8388608
  165.3 1.6 copy-done
  166.8 2.0 %copy.27 = f32[1,2048,512]{2,1,0:T(8,128)} copy(f32[1,2048,512]{2,1,0:T(8,128)S(1)} %copy-done) | data formatting | bytes 8388608
Async XLA Ops:
  152.4 6.1 %copy-start.2 = (f32[8,2,8,128]{3,2,1,0:T(8,128)S(1)}, f32[8,2,8,128]{3,2,1,0:T(8,128)}, u32[]{:S(2)}) copy-start(f32[8,2,8,128]{3,2,1,0:T(8,128)} %get-tuple-element.18) | copy-start | bytes 196612
  156.1 7.0 %copy-start.1 = (f32[1,512,2048]{2,1,0:T(8,128)S(1)}, f32[1,512,2048]{2,1,0:T(8,128)}, u32[]{:S(2)}) copy-start(f32[1,512,2048]{2,1,0:T(8,128)} %get-tuple-element.39) | copy-start | bytes 12582916
  163.1 3.7 %copy-start = (f32[1,2048,512]{2,1,0:T(8,128)S(1)}, f32[1,2048,512]{2,1,0:T(8,128)}, u32[]{:S(2)}) copy-start(f32[1,2048,512]{2,1,0:T(8,128)} %get-tuple-element.40) | copy-start | bytes 12582916

commit v2 on v1

--- a/solution.py
+++ b/solution.py
@@ -16,7 +16,7 @@
 MESH = pl.DeviceIdType.MESH
 F32 = jnp.float32
 BF16 = jnp.bfloat16
-SEMS = 176
+SEMS = 288
 
 
 def mm(a, b):
@@ -50,10 +50,10 @@
     tokens_out, token_grad, reduced, small_out, grad_in, grad_back,
     send_sem, recv_sem, local_sem,
     x_full, cot, ids_send, ids_own, wq, wk, wv, wo, win, wback,
-    attn_in, qs, ks, vs, probs, bias, linv, attn, attn_other, resid, mix_in, wc, weights, coef,
+    attn_in, qs, ks, vs, bias, linv, attn, attn_other, resid, mix_in, wc, weights, coef,
     rows_send, rows_all, back_send, back_recv, out_send, mixgrad, gresid, gbranch, gheads,
     acc_k, acc_v, act_q, act_k, act_v, part_send, part_recv, tgrad_send, pay, rs1, red1, rs2, red2, ag1,
-    small_pay, small_rs1, small_sib, small_dp, small_fin, acc_b, acc_i,
+    small_pay, small_rs1, small_sib, small_dp, small_fin, hid, gpr, out_b, out_i,
 ):
     d, g = lax.axis_index("dp"), lax.axis_index("grp")
     nc, ny = ng // 2, ndp // nx
@@ -119,7 +119,25 @@
     for b in range(nc):
         ids_send[b] = jnp.zeros((8, 128), jnp.int32)
         ids_send[b, :, 0:BLOCK] = jnp.broadcast_to(group_ids[b : b + 1, :], (8, BLOCK))
-    pl.semaphore_wait(barrier, ng + ndp - 2)
+    nz = nc // 2
+    dx, dy = d // ny, d % ny
+    xh, z = c // nz, c % nz
+    plane_a, plane_b = 2 * ndp, 2 * nc
+    at_a, at_b = xh * ndp + d, dx * nc + c
+
+    def device_a(a):
+        return {"dp": a % ndp, "grp": (a // ndp * nz + z) * 2 + p}
+
+    def device_b(b):
+        return {"dp": b // nc * ny + dy, "grp": b % nc * 2 + p}
+
+    for k in range(1, ndp):
+        far = {"dp": lax.rem(d + k, ndp), "grp": ((1 - xh) * nz + z) * 2 + p}
+        pl.semaphore_signal(barrier, inc=1, device_id=far, device_id_type=MESH)
+    for k in range(1, nc):
+        far = {"dp": (1 - dx) * ny + dy, "grp": chip_at(k) * 2 + p}
+        pl.semaphore_signal(barrier, inc=1, device_id=far, device_id_type=MESH)
+    pl.semaphore_wait(barrier, 2 * ndp + ng + nc - 4)
 
     n_tok = [number() for _ in range(nc)]
     n_fwd = [number() for _ in range(nc)]
@@ -154,7 +172,7 @@
         lax.broadcasted_iota(jnp.int32, (ng, cols), 1) // (2 * nc)
         == lax.broadcasted_iota(jnp.int32, (ng, cols), 0)
     ).astype(F32)
-    wc[...] = mm(w_ctrl[...].astype(F32), spread).astype(BF16)
+    wc[...] = mm_tn(w_ctrl[...].astype(F32), spread).astype(BF16)
 
     for k in range(1, nc):
         block = x_full.at[chip_from(k), p]
@@ -194,38 +212,43 @@
         MASKED,
     )
 
-    def key_range(i):
-        return max(length // 2, (i + 1) * q_rows)
+    def pieces(i):
+        end = (i + 1) * q_rows
+        return [(0, hl)] + ([(hl, end - hl)] if end > hl else [])
+
+    def held(head, i, n):
+        span = slice(n * length + i * q_rows, n * length + (i + 1) * q_rows)
+        return hid.at[head, span, : pieces(i)[n][1]]
 
     def rows_of(ref, i, n, pair):
         return ref[i : i + n, :, :, pair * 128 : pair * 128 + 128].reshape(n * 2 * BLOCK, 128)
 
     n_mix = number()
     for i in range(n_q):
-        extent = key_range(i)
-        blocks = extent // (2 * BLOCK)
         for pair in range(2):
             q = rows_of(qs, i * per_q, per_q, pair)
-            k_ = rows_of(ks, 0, blocks, pair)
-            v_ = rows_of(vs, 0, blocks, pair)
             outs, invs = [], []
             for h in range(2):
-                s = mm_nt(q * keep[h], k_)
-                if (i + 1) * q_rows <= hl:
-                    parts = [s + bias[i * q_rows : (i + 1) * q_rows, :]]
-                else:
-                    parts = [s[:, : extent - q_rows], s[:, extent - q_rows :] + causal]
+                parts = []
+                for start, size in pieces(i):
+                    k_ = rows_of(ks, start // (2 * BLOCK), size // (2 * BLOCK), pair)
+                    s = mm_nt(q * keep[h], k_)
+                    if (i + 1) * q_rows <= hl:
+                        s = s + bias[i * q_rows : (i + 1) * q_rows, :]
+                    elif start == hl:
+                        last = s[:, size - q_rows :] + causal
+                        s = last if size == q_rows else jnp.concatenate([s[:, : size - q_rows], last], axis=1)
+                    parts.append(s)
                 top = functools.reduce(
                     jnp.maximum, [jnp.max(part, axis=-1, keepdims=True) for part in parts]
                 )
-                at = 0
-                for part in parts:
-                    probs[pair * 2 + h, i * q_rows : (i + 1) * q_rows, at : at + part.shape[1]] = jnp.exp(part - top).astype(BF16)
-                    at += part.shape[1]
-                o = mm(
-                    probs[pair * 2 + h, i * q_rows : (i + 1) * q_rows, :extent],
-                    v_ * keep[h] + keep[1 - h],
-                )
+                o = None
+                for n, (start, size) in enumerate(pieces(i)):
+                    low = jnp.exp(parts[n] - top).astype(BF16)
+                    held(pair * 2 + h, i, n)[...] = low
+                    v_ = rows_of(vs, start // (2 * BLOCK), size // (2 * BLOCK), pair)
+                    term = mm(low, v_ * keep[h] + keep[1 - h])
+                    o = term if o is None else o + term
                 inv = 1.0 / pltpu.roll(o, HEAD_DIM, 1)
                 outs.append(o * inv)
                 invs.append(inv)
@@ -279,24 +302,67 @@
     w256 = exponent / jnp.sum(exponent, axis=0, keepdims=True)
     weights[...] = w256
     coef[...] = w256.astype(BF16)
-    rows_send[0] = mm_tn(coef[...], mix_in[...]).astype(BF16).reshape(ng, 2 * nc, width)
     cot_rows = cot[...].reshape(own, width)
-    rows_send[1] = mm_tn(coef[...], cot_rows).astype(BF16).reshape(ng, 2 * nc, width)
-
-    n_rows = [number() for _ in range(ng)]
-    for k in range(1, ng):
-        to = lax.rem(g + k, ng)
-        send(n_rows[k], rows_send.at[:, to], rows_all.at[d, :, g], grp=to)
-    rows_all[d, :, g] = rows_send[:, g]
+
     load_in.wait()
     load_back.wait()
-    for k in range(1, ng):
-        arrived(n_rows[k], rows_all.at[d, :, lax.rem(g + ng - k, ng)])
-
-    dx, dy = d // ny, d % ny
+    n_rows = [[number() for _ in range(ng)] for _ in range(2)]
+    for kind, source in enumerate((mix_in[...], cot_rows)):
+        rows_send[kind] = mm_tn(coef[...], source).astype(BF16).reshape(ng, 2 * nc, width)
+        for k in range(1, ng):
+            to = lax.rem(g + k, ng)
+            send(n_rows[kind][k], rows_send.at[kind, to], rows_all.at[d, kind, g], grp=to)
+        rows_all[d, kind, g] = rows_send[kind, g]
+
+    def rows_arrived(kind):
+        for k in range(1, ng):
+            arrived(n_rows[kind][k], rows_all.at[d, kind, lax.rem(g + ng - k, ng)])
+
+    rows_arrived(0)
+
+    tile = min(512, ff)
+    n_f = ff // tile
+    n_back = [[number() for _ in range(ng)] for _ in range(2)]
+
+    def send_back(kind, rows):
+        back_send[kind] = rows.astype(BF16).reshape(ng, 2 * nc, width)
+        for k in range(1, ng):
+            to = lax.rem(g + k, ng)
+            send(n_back[kind][k], back_send.at[kind, to], back_recv.at[kind, g], grp=to)
+        back_recv[kind, g] = back_send[kind, g]
+
+    def back_arrived(kind):
+        for k in range(1, ng):
+            arrived(n_back[kind][k], back_recv.at[kind, lax.rem(g + ng - k, ng)])
+
+    def silu_and_slope(pre):
+        sig = 0.5 + 0.5 * jnp.tanh(0.5 * pre)
+        silu = pre * sig
+        return silu, sig + silu * (1.0 - sig)
+
+    mixed = rows_all[d, 0].reshape(cols, width)
+    e_out, slopes = None, []
+    for f in range(n_f):
+        at = slice(f * tile, (f + 1) * tile)
+        silu, slope = silu_and_slope(mm(mixed, win[:, at]))
+        slopes.append(slope)
+        part = mm(silu.astype(BF16), wback[at, :])
+        e_out = part if e_out is None else e_out + part
+    send_back(0, e_out)
+
+    rows_arrived(1)
+    gexp = rows_all[d, 1].reshape(cols, width)
+    g_mixed = None
+    for f in range(n_f):
+        at = slice(f * tile, (f + 1) * tile)
+        gpre = (mm_nt(gexp, wback[at, :]) * slopes[f]).astype(BF16)
+        part = mm_nt(gpre, win[:, at])
+        g_mixed = part if g_mixed is None else g_mixed + part
+    send_back(1, g_mixed)
+
     n_m = [[number() for _ in range(ny)] for _ in range(nx)]
     n_g = [[number() for _ in range(ny)] for _ in range(nx)]
-    x_to = (1 - dx) * ny + dy if nx == 2 else d
+    x_to = (1 - dx) * ny + dy
 
     def y_at(k, x):
         return x * ny + lax.rem(dy + k, ny)
@@ -304,59 +370,24 @@
     def y_from(k, x):
         return x * ny + lax.rem(dy + ny - k, ny)
 
-    if nx == 2:
-        send(n_m[1][0], rows_all.at[d, 0], rows_all.at[d, 0], dp=x_to)
+    send(n_m[1][0], rows_all.at[d, 0], rows_all.at[d, 0], dp=x_to)
     for k in range(1, ny):
         send(n_g[0][k], rows_all.at[d, 1], rows_all.at[d, 1], dp=y_at(k, dx))
         send(n_m[0][k], rows_all.at[d, 0], rows_all.at[d, 0], dp=y_at(k, dx))
-    if nx == 2:
-        send(n_g[1][0], rows_all.at[d, 1], rows_all.at[d, 1], dp=x_to)
-
-    mixed = rows_all[d, 0].reshape(cols, width)
-    gexp = rows_all[d, 1].reshape(cols, width)
-    tile = min(512, ff)
-
-    def expert_tile(f, mixed, gexp):
-        at = pl.ds(pl.multiple_of(f * tile, tile), tile)
-        w1, w2 = win[:, at], wback[at, :]
-        pre = mm(mixed, w1)
-        sig = jax.nn.sigmoid(pre)
-        hidden = (pre * sig).astype(BF16)
-        ghid = mm_nt(gexp, w2)
-        gpre = (ghid * (sig * (1.0 + pre * (1.0 - sig)))).astype(BF16)
-        return hidden, gpre, w1, w2
-
-    e_out = g_mixed = None
-    for f in range(ff // tile):
-        hidden, gpre, w1, w2 = expert_tile(f, mixed, gexp)
-        e_part, g_part = mm(hidden, w2), mm_nt(gpre, w1)
-        e_out = e_part if e_out is None else e_out + e_part
-        g_mixed = g_part if g_mixed is None else g_mixed + g_part
-    back_send[0] = e_out.astype(BF16).reshape(ng, 2 * nc, width)
-    back_send[1] = g_mixed.astype(BF16).reshape(ng, 2 * nc, width)
-    n_back = [number() for _ in range(ng)]
-    for k in range(1, ng):
-        to = lax.rem(g + k, ng)
-        send(n_back[k], back_send.at[:, to], back_recv.at[:, g], grp=to)
-    back_recv[:, g] = back_send[:, g]
-
-    if nx == 2:
-        from_x = rows_all.at[x_to, 0]
-        arrived(n_m[1][0], from_x)
-        for k in range(1, ny):
-            send(n_m[1][k], from_x, from_x, dp=y_at(k, dx))
-    for k in range(1, ng):
-        arrived(n_back[k], back_recv.at[:, lax.rem(g + ng - k, ng)])
-
+    send(n_g[1][0], rows_all.at[d, 1], rows_all.at[d, 1], dp=x_to)
+
+    back_arrived(0)
     e_rows = back_recv[0].reshape(cols, width)
-    g_rows = back_recv[1].reshape(cols, width)
     out_send[...] = (resid[...] + mm(coef[...], e_rows)).astype(BF16).reshape(nc, BLOCK, width)
     n_out = [number() for _ in range(nc)]
     for k in range(1, nc):
         to = chip_at(k)
         send(n_out[k], out_send.at[to], tokens_out.at[c], grp=to * 2 + p)
     keep_out = local(out_send.at[c], tokens_out.at[c])
-    dots = mm_nt(cot_rows, e_rows) + mm_nt(mix_in[...], g_rows)
+    dots = mm_nt(cot_rows, e_rows)
+    back_arrived(1)
+    g_rows = back_recv[1].reshape(cols, width)
+    dots = dots + mm_nt(mix_in[...], g_rows)
     w256 = weights[...]
     inner = jnp.sum(w256 * dots, axis=0, keepdims=True)
     glogit = (w256 * (dots - inner)).astype(BF16)
@@ -395,38 +426,42 @@
     arrived(n_branch, gbranch.at[oth])
     head_grads(oth)
 
-    if nx == 2:
+    from_x = rows_all.at[x_to, 0]
+    arrived(n_m[1][0], from_x)
+    for k in range(1, ny):
+        send(n_m[1][k], from_x, from_x, dp=y_at(k, dx))
+
+    def second_hop():
         arrived(n_g[1][0], rows_all.at[x_to, 1])
         for k in range(1, ny):
             block = rows_all.at[y_from(k, dx), 1]
             arrived(n_g[0][k], block)
             send(n_g[1][k], block, block, dp=x_to)
-    else:
-        for k in range(1, ny):
-            arrived(n_g[0][k], rows_all.at[y_from(k, dx), 1])
 
     acc_k[...] = jnp.zeros_like(acc_k)
     acc_v[...] = jnp.zeros_like(acc_v)
     for i in range(n_q):
-        extent = key_range(i)
-        blocks = extent // (2 * BLOCK)
-        span = slice(i * q_rows, (i + 1) * q_rows)
+        if i == n_q - 1:
+            second_hop()
         for pair in range(2):
             at = slice(pair * 128, pair * 128 + 128)
             q = rows_of(qs, i * per_q, per_q, pair)
-            k_ = rows_of(ks, 0, blocks, pair)
-            v_ = rows_of(vs, 0, blocks, pair)
-            grads, dqs = [], []
+            dqs = []
             for h in range(2):
                 up = gheads[pair * 2 + h, i * per_q : (i + 1) * per_q].reshape(q_rows, 128)
-                dp = mm_nt(up, v_ * keep[h] + keep[1 - h]).astype(BF16)
-                ds = probs[pair * 2 + h, span, :extent] * dp
-                grads.append(up * keep[h])
-                dqs.append(mm(ds, k_))
-                part_k = mm_tn(ds, q * keep[h])
-                part_v = mm_tn(probs[pair * 2 + h, span, :extent], grads[h])
-                acc_k[:extent, at] += part_k
-                acc_v[:extent, at] += part_v
+                up_only = up * keep[h]
+                q_only = q * keep[h]
+                dq = None
+                for n, (start, size) in enumerate(pieces(i)):
+                    k_ = rows_of(ks, start // (2 * BLOCK), size // (2 * BLOCK), pair)
+                    v_ = rows_of(vs, start // (2 * BLOCK), size // (2 * BLOCK), pair)
+                    prob = held(pair * 2 + h, i, n)[...]
+                    ds = prob * mm_nt(up, v_ * keep[h] + keep[1 - h]).astype(BF16)
+                    term = mm(ds, k_)
+                    dq = term if dq is None else dq + term
+                    acc_k[start : start + size, at] += mm_tn(ds, q_only)
+                    acc_v[start : start + size, at] += mm_tn(prob, up_only)
+                dqs.append(dq)
             act_q[i * per_q : (i + 1) * per_q, :, :, at] = (
                 (jnp.where(low_lane, dqs[0], dqs[1]) * HEAD_DIM**-0.5)
                 .astype(BF16)
@@ -447,19 +482,40 @@
     mixgrad[...] = act_grad(p)
 
     a = attn_in[...].reshape(length, width)
+    out_part = sum(
+        mm_tn(attn[:, par].reshape(own, half), gbranch[par].reshape(own, width)) for par in range(2)
+    ).astype(BF16)
+    n_red = 2
+    firsts = (nz, ny)
+    planes = (plane_a, plane_b)
+    here_1, here_2 = (z, dy), (at_a, at_b)
+    device_2 = (device_a, device_b)
+
+    def device_1(r, to):
+        return {"grp": (xh * nz + to) * 2 + p} if r == 0 else {"dp": dx * ny + to}
+
     for part, act in enumerate((act_q, act_k, act_v)):
         grad = mm_tn(a, act[...].reshape(length, half)).astype(BF16)
-        pay[part * half : (part + 1) * half, :half] = grad[:half]
-        pay[part * half : (part + 1) * half, half:] = grad[half:]
-    pay[3 * half : 4 * half, :] = sum(
-        mm_tn(attn[:, par].reshape(own, half), gbranch[par].reshape(own, width)) for par in range(2)
-    ).astype(BF16)
-    ra = 4 * half // nc
-    rb = ra // ndp
-    n_rs1 = [number() for _ in range(nc)]
-    for k in range(1, nc):
-        to = chip_at(k)
-        send(n_rs1[k], pay.at[pl.ds(pl.multiple_of(to * ra, ra), ra)], rs1.at[c], grp=to * 2 + p)
+        for r in range(n_red):
+            n1, sub = firsts[r], planes[r] // 4
+            rows = half // n1
+            for j in range(n1):
+                pay[r, j, part * sub : (part + 1) * sub] = grad[
+                    r * half + j * rows : r * half + (j + 1) * rows
+                ].reshape(sub, rows // sub, half)
+    for r in range(n_red):
+        n1, sub = firsts[r], planes[r] // 4
+        rows = half // n1
+        for j in range(n1):
+            pay[r, j, 3 * sub : 4 * sub] = out_part[
+                j * rows : (j + 1) * rows, r * half : (r + 1) * half
+            ].reshape(sub, rows // sub, half)
+    n_rs1 = [[number() for _ in range(firsts[r])] for r in range(n_red)]
+    for k in range(1, max(firsts)):
+        for r in range(n_red):
+            if k < firsts[r]:
+                to = lax.rem(here_1[r] + k, firsts[r])
+                send(n_rs1[r][k], pay.at[r, to], rs1.at[r, here_1[r]], **device_1(r, to))
 
     arrived(n_part, part_recv)
 
@@ -495,121 +551,158 @@
         to = chip_at(k)
         send(n_s1[k], small_pay.at[to], small_rs1.at[c], grp=to * 2 + p)
     small_rs1[c] = small_pay[c]
-    rs1[c] = pay[pl.ds(pl.multiple_of(c * ra, ra), ra), :]
-
-    for k in range(1, nc):
-        arrived(n_rs1[k], rs1.at[chip_from(k)])
-    total = rs1[0].astype(F32)
-    for j in range(1, nc):
-        total = total + rs1[j].astype(F32)
-    red1[...] = total.astype(BF16)
-    n_rs2 = [number() for _ in range(ndp)]
-    for k in range(1, ndp):
-        to = lax.rem(d + k, ndp)
-        send(n_rs2[k], red1.at[pl.ds(pl.multiple_of(to * rb, rb), rb)], rs2.at[d], dp=to)
-    rs2[d] = red1[pl.ds(pl.multiple_of(d * rb, rb), rb), :]
+
+    def hidden_rows(x):
+        def body(f, carry):
+            at = pl.ds(pl.multiple_of(f * tile, tile), tile)
+            m_rows = rows_all[pl.ds(x * ny, ny), 0].reshape(ny * cols, width)
+            g_rows = rows_all[pl.ds(x * ny, ny), 1].reshape(ny * cols, width)
+            rows = pl.ds(pl.multiple_of(x * ny * cols, ny * cols), ny * cols)
+            silu, slope = silu_and_slope(mm(m_rows, win[:, at]))
+            hid[f, rows, :] = silu.astype(BF16)
+            gpr[f, rows, :] = (mm_nt(g_rows, wback[at, :]) * slope).astype(BF16)
+            return carry
+
+        lax.fori_loop(0, n_f, body, 0)
+
+    stores = []
+
+    def weight_grads(f):
+        slot = f % 2
+        if f >= 2:
+            for copy in stores[f - 2]:
+                copy.wait()
+        m_rows = rows_all[:, 0].reshape(ndp * cols, width)
+        g_rows = rows_all[:, 1].reshape(ndp * cols, width)
+        out_b[slot] = mm_tn(hid[f], g_rows).astype(BF16)
+        out_i[slot] = mm_tn(m_rows, gpr[f]).astype(BF16)
+        stores.append(
+            (
+                local(out_b.at[slot], grad_back.at[0, f * tile : (f + 1) * tile, :]),
+                local(out_i.at[slot], grad_in.at[0, :, f * tile : (f + 1) * tile]),
+            )
+        )
+
+    for k in range(1, ny):
+        arrived(n_m[0][k], rows_all.at[y_from(k, dx), 0])
+    hidden_rows(dx)
+
+    n_rs2 = [[number() for _ in range(planes[r])] for r in range(n_red)]
+    for r in range(n_red):
+        for k in range(1, firsts[r]):
+            arrived(n_rs1[r][k], rs1.at[r, lax.rem(here_1[r] + firsts[r] - k, firsts[r])])
+        rs1[r, here_1[r]] = pay[r, here_1[r]]
+        total = rs1[r, 0].astype(F32)
+        for j in range(1, firsts[r]):
+            total = total + rs1[r, j].astype(F32)
+        red1[r] = total.astype(BF16)
+        for k in range(1, planes[r]):
+            to = lax.rem(here_2[r] + k, planes[r])
+            send(n_rs2[r][k], red1.at[r, to], rs2.at[r, here_2[r]], **device_2[r](to))
+        rs2[r, here_2[r]] = red1[r, here_2[r]]
     for k in range(1, nc):
         arrived(n_s1[k], small_rs1.at[chip_from(k)])
     small_sib[p] = small_rs1[...].sum(axis=0)
     n_ss = number()
     send(n_ss, small_sib.at[p], small_sib.at[p], grp=sib)
 
-    if nx == 2:
-        for k in range(1, ny):
-            arrived(n_g[1][k], rows_all.at[y_from(k, 1 - dx), 1])
-            arrived(n_m[1][k], rows_all.at[y_from(k, 1 - dx), 0])
     for k in range(1, ny):
-        arrived(n_m[0][k], rows_all.at[y_from(k, dx), 0])
-
-    for k in range(1, ndp):
-        arrived(n_rs2[k], rs2.at[lax.rem(d + ndp - k, ndp)])
-    total = rs2[0].astype(F32)
-    for j in range(1, ndp):
-        total = total + rs2[j].astype(F32)
-    red2[...] = total.astype(BF16)
-    n_ag1 = [number() for _ in range(ndp)]
-    mine = ag1.at[pl.ds(pl.multiple_of(d * rb, rb), rb)]
-    for k in range(1, ndp):
-        send(n_ag1[k], red2, mine, dp=lax.rem(d + k, ndp))
-    ag1[pl.ds(pl.multiple_of(d * rb, rb), rb), :] = red2[...]
+        arrived(n_g[1][k], rows_all.at[y_from(k, 1 - dx), 1])
+        arrived(n_m[1][k], rows_all.at[y_from(k, 1 - dx), 0])
+    hidden_rows(1 - dx)
+
+    n_ag1 = [[number() for _ in range(planes[r])] for r in range(n_red)]
+    for r in range(n_red):
+        for k in range(1, planes[r]):
+            arrived(n_rs2[r][k], rs2.at[r, lax.rem(here_2[r] + planes[r] - k, planes[r])])
+        total = rs2[r, 0].astype(F32)
+        for j in range(1, planes[r]):
+            total = total + rs2[r, j].astype(F32)
+        red2[r] = total.astype(BF16)
+        for k in range(1, planes[r]):
+            to = lax.rem(here_2[r] + k, planes[r])
+            send(n_ag1[r][k], red2.at[r], ag1.at[r, here_2[r]], **device_2[r](to))
+        ag1[r, here_2[r]] = red2[r]
     arrived(n_ss, small_sib.at[oth])
     small_dp[d] = small_sib[0] + small_sib[1]
     n_sd = [number() for _ in range(ndp)]
     for k in range(1, ndp):
         send(n_sd[k], small_dp.at[d], small_dp.at[d], dp=lax.rem(d + k, ndp))
 
-    step = min(2, ndp)
-    n_half = 2
-    for f in range(ff // tile):
-        if f == 1:
-            for k in range(1, ndp):
-                frm = lax.rem(d + ndp - k, ndp)
-                arrived(n_ag1[k], ag1.at[pl.ds(pl.multiple_of(frm * rb, rb), rb)])
-            n_ag2 = [number() for _ in range(nc)]
-            n_ag3 = [number() for _ in range(nc)]
-            place_c = reduced.at[p, pl.ds(pl.multiple_of(c * ra, ra), ra)]
-            for k in range(1, nc):
-                send(n_ag2[k], ag1, place_c, grp=chip_at(k) * 2 + p)
-            send(n_ag3[0], ag1, place_c, grp=sib)
-            keep_red = local(ag1, place_c)
-            for k in range(1, ndp):
-                arrived(n_sd[k], small_dp.at[lax.rem(d + ndp - k, ndp)])
-            small_fin[...] = small_dp[...].sum(axis=0)
-            n_sg = [number() for _ in range(nc)]
-            for k in range(1, nc):
-                send(n_sg[k], small_fin, small_out.at[c], grp=chip_at(k) * 2 + p)
-            keep_small = local(small_fin, small_out.at[c])
-        if f == ff // tile - 1:
-            for k in range(1, nc):
-                place_k = reduced.at[p, pl.ds(pl.multiple_of(chip_from(k) * ra, ra), ra)]
-                arrived(n_ag2[k], place_k)
-                send(n_ag3[k], place_k, place_k, grp=sib)
-        slot = f % n_half
-
-        def chunk(j, carry, f=f, slot=slot):
-            m_rows = rows_all[pl.ds(j * step, step), 0].reshape(step * cols, width)
-            g_rows = rows_all[pl.ds(j * step, step), 1].reshape(step * cols, width)
-            hidden, gpre, _, _ = expert_tile(f, m_rows, g_rows)
-            part_b, part_i = mm_tn(hidden, g_rows), mm_tn(m_rows, gpre)
-
-            @pl.when(j == 0)
-            def _():
-                acc_b[slot] = part_b
-                acc_i[slot] = part_i
-
-            @pl.when(j > 0)
-            def _():
-                acc_b[slot] += part_b
-                acc_i[slot] += part_i
-
-            return carry
-
-        if f >= n_half:
-            stores[f - n_half][0].wait()
-            stores[f - n_half][1].wait()
-        else:
-            stores = [] if f == 0 else stores
-        lax.fori_loop(0, ndp // step, chunk, 0)
-        stores.append(
-            (
-                local(acc_b.at[slot], grad_back.at[0, f * tile : (f + 1) * tile, :]),
-                local(acc_i.at[slot], grad_in.at[0, :, f * tile : (f + 1) * tile]),
-            )
-        )
-
-    for b, i in stores[-n_half:]:
-        b.wait()
-        i.wait()
+    for f in range(n_f // 2):
+        weight_grads(f)
+
+    n_ag2 = [[number() for _ in range(firsts[r])] for r in range(n_red)]
+    n_ag3 = [[number() for _ in range(firsts[r])] for r in range(n_red)]
+    keep_red = []
+    for r in range(n_red):
+        for k in range(1, planes[r]):
+            arrived(n_ag1[r][k], ag1.at[r, lax.rem(here_2[r] + planes[r] - k, planes[r])])
+        place = reduced.at[p, r, here_1[r]]
+        for k in range(1, firsts[r]):
+            to = lax.rem(here_1[r] + k, firsts[r])
+            send(n_ag2[r][k], ag1.at[r], place, **device_1(r, to))
+        send(n_ag3[r][0], ag1.at[r], place, grp=sib)
+        keep_red.append(local(ag1.at[r], place))
+    for k in range(1, ndp):
+        arrived(n_sd[k], small_dp.at[lax.rem(d + ndp - k, ndp)])
+    small_fin[...] = small_dp[...].sum(axis=0)
+    n_sg = [number() for _ in range(nc)]
+    for k in range(1, nc):
+        send(n_sg[k], small_fin, small_out.at[c], grp=chip_at(k) * 2 + p)
+    keep_small = local(small_fin, small_out.at[c])
+
+    for f in range(n_f // 2, n_f):
+        weight_grads(f)
+
+    for k in range(1, max(firsts)):
+        for r in range(n_red):
+            if k < firsts[r]:
+                place = reduced.at[p, r, lax.rem(here_1[r] + firsts[r] - k, firsts[r])]
+                arrived(n_ag2[r][k], place)
+                send(n_ag3[r][k], place, place, grp=sib)
+    for pair in stores[-2:]:
+        for copy in pair:
+            copy.wait()
     for k in range(1, nc):
         arrived(n_out[k], tokens_out.at[chip_from(k)])
         arrived(n_tg[k], token_grad.at[chip_from(k)])
         arrived(n_sg[k], small_out.at[chip_from(k)])
-    for k in range(nc):
-        arrived(n_ag3[k], reduced.at[oth, pl.ds(pl.multiple_of(chip_from(k) * ra, ra), ra)])
-    for copy in (keep_out, keep_tg, keep_red, keep_small):
+    for r in range(n_red):
+        for k in range(firsts[r]):
+            arrived(n_ag3[r][k], reduced.at[oth, r, lax.rem(here_1[r] + firsts[r] - k, firsts[r])])
+    for copy in [keep_out, keep_tg, keep_small] + keep_red:
         copy.wait()
     for copy in started:
         copy.wait_send()
+
+
+def finish_kernel(
+    tokens_out, token_grad, reduced, small, grad_in, grad_back,
+    out_tokens, out_tgrad, out_qkv, out_out, out_gain_a, out_gain_m, out_ctrl, out_in, out_back,
+):
+    tiles = small.shape[1] - 1
+    width = out_out.shape[2] * 2
+    half = width // 2
+    out_tokens[...] = tokens_out[...]
+    out_tgrad[...] = token_grad[...].astype(F32)
+    out_in[...] = grad_in[...].astype(F32)
+    out_back[...] = grad_back[...].astype(F32)
+    rows = out_qkv.shape[0]
+    sub = reduced.shape[3] // 4
+    for p in range(2):
+        for part in range(3):
+            at = part * width + p * half
+            out_qkv[:, at : at + half] = (
+                reduced[p, 0, 0, part * sub : (part + 1) * sub].reshape(rows, half).astype(F32)
+            )
+        out_out[p] = reduced[p, 0, 0, 3 * sub : 4 * sub].reshape(rows, half).astype(F32)
+    for l in range(4):
+        at = slice(l * 128, l * 128 + 128)
+        out_gain_a[:, at] = small[0, tiles, l : l + 1]
+        out_gain_m[:, at] = small[0, tiles, 4 + l : 5 + l]
+    for j in range(8):
+        out_ctrl[j // 4 * 8 : j // 4 * 8 + 8, j % 4 * 128 : j % 4 * 128 + 128] = small[j // tiles, j % tiles]
 
 
 def on_device(
@@ -622,7 +715,7 @@
     length, own = ng * BLOCK, nc * BLOCK
     ff = w_in.shape[2]
     cols = ng * 2 * nc
-    ra = 4 * half // nc
+    n1, plane = nc // 2, 2 * nc
     tile = min(512, ff)
     tiles = 8 // nc
     vm = pltpu.VMEM
@@ -647,7 +740,6 @@
         vm((nc, 2, BLOCK, half), BF16),
         vm((nc, 2, BLOCK, half), BF16),
         vm((nc, 2, BLOCK, half), BF16),
-        vm((4, length, length), BF16),
         vm((length // 2, length // 2), F32),
         vm((nc, 2, BLOCK, half), F32),
         vm((nc, 2, BLOCK, half), BF16),
@@ -674,29 +766,31 @@
         vm((nc, BLOCK, width), BF16),
         vm((nc, BLOCK, width), BF16),
         vm((nc, BLOCK, width), BF16),
-        vm((4 * half, width), BF16),
-        vm((nc, ra, width), BF16),
-        vm((ra, width), BF16),
-        vm((ndp, ra // ndp, width), BF16),
-        vm((ra // ndp, width), BF16),
-        vm((ra, width), BF16),
+        vm((2, n1, plane, 16, half), BF16),
+        vm((2, n1, plane, 16, half), BF16),
+        vm((2, plane, 16, half), BF16),
+        vm((2, plane, 16, half), BF16),
+        vm((2, 16, half), BF16),
+        vm((2, plane, 16, half), BF16),
         vm((nc, tiles + 1, 8, 128), F32),
         vm((nc, tiles + 1, 8, 128), F32),
         vm((2, tiles + 1, 8, 128), F32),
         vm((ndp, tiles + 1, 8, 128), F32),
         vm((tiles + 1, 8, 128), F32),
-        vm((2, tile, width), F32),
-        vm((2, width, tile), F32),
+        vm((ff // tile, ndp * cols, tile), BF16),
+        vm((ff // tile, ndp * cols, tile), BF16),
+        vm((2, tile, width), BF16),
+        vm((2, width, tile), BF16),
     ]
     tokens_out, token_grad, reduced, small, grad_in, grad_back = pl.pallas_call(
         functools.partial(block_kernel, ng, ndp, nx),
         out_shape=[
             jax.ShapeDtypeStruct(tokens.shape, BF16),
             jax.ShapeDtypeStruct(tokens.shape, BF16),
-            jax.ShapeDtypeStruct((2, 4 * half, width), BF16),
+            jax.ShapeDtypeStruct((2, 2, n1, plane, 16, half), BF16),
             jax.ShapeDtypeStruct((nc, tiles + 1, 8, 128), F32),
-            jax.ShapeDtypeStruct(w_in.shape, F32),
-            jax.ShapeDtypeStruct(w_back.shape, F32),
+            jax.ShapeDtypeStruct(w_in.shape, BF16),
+            jax.ShapeDtypeStruct(w_back.shape, BF16),
         ],
         in_specs=[anywhere] * 4 + [in_vmem] * 3 + [anywhere] * 2 + [in_smem, in_vmem],
         out_specs=[anywhere] * 6,
@@ -707,23 +801,54 @@
         name="of_tokens_block",
     )(
         tokens, cotangent, w_qkv, w_out.reshape(2, half, width), gain_attn.reshape(1, width),
-        gain_mix.reshape(1, width), w_ctrl, w_in, w_back, prefix, group_ids,
+        gain_mix.reshape(1, width), w_ctrl.T, w_in, w_back, prefix, group_ids,
     )
-    halves = reduced.reshape(2, 4, half, 2, half)
-    grad_qkv = halves[:, :3].transpose(3, 2, 1, 0, 4).reshape(width, 3 * width).astype(F32)
-    grad_out = reduced[:, 3 * half :].reshape(width, width).astype(F32)
-    ctrl_tiles = small[:, :tiles].reshape(2, 4, 8, 128).transpose(0, 2, 1, 3).reshape(16, width)
-    grad_ctrl = ctrl_tiles[:ng].T
-    grad_gain_attn = small[0, tiles, :4].reshape(width)
-    grad_gain_mix = small[0, tiles, 4:].reshape(width)
+    steps = 2 * n1
+
+    def whole(shape):
+        return pl.BlockSpec(shape, lambda s: (0,) * len(shape))
+
+    def split(shape, axis):
+        block = tuple(n // steps if i == axis else n for i, n in enumerate(shape))
+        return pl.BlockSpec(block, lambda s: tuple(s if i == axis else 0 for i in range(len(shape))))
+
+    shapes = [
+        (tokens.shape, BF16), (tokens.shape, F32), ((width, 3 * width), F32), ((2, half, width), F32),
+        ((1, width), F32), ((1, width), F32), ((16, width), F32), (w_in.shape, F32), (w_back.shape, F32),
+    ]
+    tokens_out, token_grad, grad_qkv, grad_out, gain_a, gain_m, ctrl, grad_in, grad_back = pl.pallas_call(
+        finish_kernel,
+        grid=(steps,),
+        out_shape=[jax.ShapeDtypeStruct(*shape) for shape in shapes],
+        in_specs=[
+            split(tokens.shape, 0),
+            split(tokens.shape, 0),
+            pl.BlockSpec((2, 1, 1, plane, 16, half), lambda s: (0, s // n1, s % n1, 0, 0, 0)),
+            whole(small.shape),
+            split(w_in.shape, 1),
+            split(w_back.shape, 1),
+        ],
+        out_specs=[
+            split(tokens.shape, 0),
+            split(tokens.shape, 0),
+            split((width, 3 * width), 0),
+            pl.BlockSpec((2, half // n1, half), lambda s: (0, s % n1, s // n1)),
+            whole((1, width)),
+            whole((1, width)),
+            whole((16, width)),
+            split(w_in.shape, 1),
+            split(w_back.shape, 1),
+        ],
+        name="finish",
+    )(tokens_out, token_grad, reduced, small, grad_in, grad_back)
     return (
         tokens_out,
-        token_grad.astype(F32),
+        token_grad,
         grad_qkv,
-        grad_out,
-        grad_gain_attn,
-        grad_gain_mix,
-        grad_ctrl,
+        grad_out.reshape(width, width),
+        gain_a.reshape(width),
+        gain_m.reshape(width),
+        ctrl[:ng].T,
         grad_in,
         grad_back,
     )

time: 169 us -> 133 us (0.79)
  local copies, waits for them, and re-layouts: 20.9 us -> 0 us
  Pallas kernels: 143 us -> 132 us
  other arithmetic: 4.36 us -> 0 us
    pallas_call x1, Pallas kernels: 143 us -> 122 us  [on_device(): pl.pallas_call(functools.partial(block_kernel, ng, ndp, nx), out_shape=[j...]
    pallas_call x0 -> x1, Pallas kernels: none -> 9.38 us  [on_device(): pl.pallas_call(finish_kernel, grid=(steps,), out_shape=[jax.ShapeDtypeStr...]
    unnamed x10 -> x0, local copies, waits for them, and re-layouts: 9.07 us -> none
    convert_element_type x2 -> x0, local copies, waits for them, and re-layouts: 6.12 us -> none  [on_device(): halves[:, :3].transpose(3, 2, 1, 0, 4).reshape(width, 3 * width).astype(F32)]
    convert_element_type x3 -> x0, other arithmetic: 4.36 us -> none  [the longest x1 2.14 us: on_device(): token_grad.astype(F32)]
    reshape x1 -> x0, local copies, waits for them, and re-layouts: 2.55 us -> none  [on_device(): halves = reduced.reshape(2, 4, half, 2, half)]
    slice x2 -> x0, local copies, waits for them, and re-layouts: 1.84 us -> none  [the longest x1 1.23 us: on_device(): grad_out = reduced[:, 3 * half:].reshape(width, width).astype(F32)]
where the time goes in v2:
time: 133 us; the launch traced here: 132 us
  Pallas kernels  132 us (99%)
    pallas_call x1, Pallas kernels, on_device(): pl.pallas_call(functools.partial(block_kernel, ng, ndp, nx), out_shape=[j...  122 us
    pallas_call x1, Pallas kernels, on_device(): pl.pallas_call(finish_kernel, grid=(steps,), out_shape=[jax.ShapeDtypeStr...  9.38 us

profile of v2, /device:TPU:1, one launch (start us, length us, event | category | flops | bytes accessed | tf_op | source)
XLA Modules:
  0.0 132.4 jit_solution(12221951046451867777)
XLA Ops:
  0.6 122.2 %of_tokens_block.1 = (bf16[8,64,512]{2,1,0:T(8,128)(2,1)}, bf16[8,64,512]{2,1,0:T(8,128)(2,1)}, bf16[2,2,4,16,16,256]{5,4,3,2,1,0:T(8,128)(2,1)}, f32[8,2,8,128]...) custom-call(bf16[8,64,512]{2,1,0:T(8,128)(2,1)} %tokens.1, ...), custom_call_target="tpu_custom_call" | custom-call | tf_op jit(solution)/shard_map/of_tokens_block/pallas_call | solution.py:785
  122.8 9.4 %finish.1 = (bf16[8,64,512]{2,1,0:T(8,128)(2,1)}, f32[8,64,512]{2,1,0:T(8,128)}, f32[512,1536]{1,0:T(8,128)}, f32[2,256,512]{2,1,0:T(8,128)}, f32[1,512]{1,0:T(1...) custom-call(bf16[8,64,512]{2,1,0:T(8,128)(2,1)} %get-tuple-element.24.tokens_ou, ...), custom_call_target="tpu_custom_call" | custom-call | tf_op jit(solution)/shard_map/finish/pallas_call | solution.py:819

commit v3 on v2

--- a/solution.py
+++ b/solution.py
@@ -70,19 +70,22 @@
     per_q = q_rows // (2 * BLOCK)
     cols = ng * 2 * nc
 
-    started, used = [], [0, 0]
+    started, in_loop, used = [], [], [0, 0]
 
     def number():
         used[0] += 1
         return used[0] - 1
 
-    def send(n, src, dst, **device):
+    def send(n, src, dst, like=None, **device):
         copy = pltpu.make_async_remote_copy(
             src_ref=src, dst_ref=dst, send_sem=send_sem.at[n], recv_sem=recv_sem.at[n],
             device_id=device, device_id_type=MESH,
         )
         copy.start()
-        started.append(copy)
+        if like is None:
+            started.append(copy)
+        else:
+            in_loop.append((n, like))
 
     def arrived(n, dst):
         pltpu.make_async_remote_copy(
@@ -149,9 +152,6 @@
     for k in range(1, nc):
         to = chip_at(k)
         send(n_ids[k], ids_send.at[to], ids_own.at[c], grp=to * 2 + p)
-    for k in range(1, nc):
-        to = chip_at(k)
-        send(n_cot[k], cotangent.at[to], cot.at[c], grp=to * 2 + p)
     ids_own[c] = ids_send[c]
     load_tokens.wait()
     send(n_fwd[0], x_full.at[c, p], x_full.at[c, p], grp=sib)
@@ -178,6 +178,9 @@
         block = x_full.at[chip_from(k), p]
         arrived(n_tok[k], block)
         send(n_fwd[k], block, block, grp=sib)
+    for k in range(1, nc):
+        to = chip_at(k)
+        send(n_cot[k], cotangent.at[to], cot.at[c], grp=to * 2 + p)
     for load in loads_qkv:
         load.wait()
 
@@ -307,8 +310,17 @@
     load_in.wait()
     load_back.wait()
     n_rows = [[number() for _ in range(ng)] for _ in range(2)]
-    for kind, source in enumerate((mix_in[...], cot_rows)):
-        rows_send[kind] = mm_tn(coef[...], source).astype(BF16).reshape(ng, 2 * nc, width)
+    n_m = [[number() for _ in range(ny)] for _ in range(nx)]
+    n_g = [[number() for _ in range(ny)] for _ in range(nx)]
+    x_to = (1 - dx) * ny + dy
+
+    def y_at(k, x):
+        return x * ny + lax.rem(dy + k, ny)
+
+    def y_from(k, x):
+        return x * ny + lax.rem(dy + ny - k, ny)
+
+    def send_rows(kind):
         for k in range(1, ng):
             to = lax.rem(g + k, ng)
             send(n_rows[kind][k], rows_send.at[kind, to], rows_all.at[d, kind, g], grp=to)
@@ -318,6 +330,10 @@
         for k in range(1, ng):
             arrived(n_rows[kind][k], rows_all.at[d, kind, lax.rem(g + ng - k, ng)])
 
+    rows_send[0] = mm_tn(coef[...], mix_in[...]).astype(BF16).reshape(ng, 2 * nc, width)
+    send_rows(0)
+    rows_send[1] = mm_tn(coef[...], cot_rows).astype(BF16).reshape(ng, 2 * nc, width)
+    send_rows(1)
     rows_arrived(0)
 
     tile = min(512, ff)
@@ -359,16 +375,6 @@
         part = mm_nt(gpre, win[:, at])
         g_mixed = part if g_mixed is None else g_mixed + part
     send_back(1, g_mixed)
-
-    n_m = [[number() for _ in range(ny)] for _ in range(nx)]
-    n_g = [[number() for _ in range(ny)] for _ in range(nx)]
-    x_to = (1 - dx) * ny + dy
-
-    def y_at(k, x):
-        return x * ny + lax.rem(dy + k, ny)
-
-    def y_from(k, x):
-        return x * ny + lax.rem(dy + ny - k, ny)
 
     send(n_m[1][0], rows_all.at[d, 0], rows_all.at[d, 0], dp=x_to)
     for k in range(1, ny):
@@ -406,6 +412,46 @@
     n_branch = number()
     send(n_branch, gbranch.at[p], gbranch.at[p], grp=sib)
 
+    tiles = 8 // nc
+    for j in range(8):
+        r, l = j // 4, j % 4
+        if ng >= 8 * (r + 1):
+            small_pay[j // tiles, j % tiles] = ctrl[r * 8 : r * 8 + 8, l * 128 : l * 128 + 128]
+        else:
+            small_pay[j // tiles, j % tiles] = jnp.zeros((8, 128), F32)
+            if ng > 8 * r:
+                small_pay[j // tiles, j % tiles, : ng - 8 * r] = ctrl[r * 8 : ng, l * 128 : l * 128 + 128]
+    for j in range(nc):
+        small_pay[j, tiles] = jnp.zeros((8, 128), F32)
+        for l in range(4):
+            small_pay[j, tiles, l : l + 1] = gain_m_part[:, l * 128 : l * 128 + 128]
+    n_s1 = [number() for _ in range(nc)]
+    for k in range(1, nc):
+        to = chip_at(k)
+        send(n_s1[k], small_pay.at[to], small_rs1.at[c], grp=to * 2 + p)
+    small_rs1[c] = small_pay[c]
+    n_ss = number()
+    n_sd = [number() for _ in range(ndp)]
+    n_sg = [number() for _ in range(nc)]
+
+    def small_step(step):
+        if step == 0:
+            for k in range(1, nc):
+                arrived(n_s1[k], small_rs1.at[chip_from(k)])
+            small_sib[p] = small_rs1[...].sum(axis=0)
+            send(n_ss, small_sib.at[p], small_sib.at[p], grp=sib)
+        elif step == 1:
+            arrived(n_ss, small_sib.at[oth])
+            small_dp[d] = small_sib[0] + small_sib[1]
+            for k in range(1, ndp):
+                send(n_sd[k], small_dp.at[d], small_dp.at[d], like=lambda: small_dp.at[0], dp=lax.rem(d + k, ndp))
+        else:
+            for k in range(1, ndp):
+                arrived(n_sd[k], small_dp.at[lax.rem(d + ndp - k, ndp)])
+            small_fin[...] = small_dp[...].sum(axis=0)
+            for k in range(1, nc):
+                send(n_sg[k], small_fin, small_out.at[c], grp=chip_at(k) * 2 + p)
+
     def head_grads(par):
         raw = mm_nt(gbranch[par].reshape(own, width), wo[p])
         scaled = (raw * linv[:, par].reshape(own, half)).astype(BF16)
@@ -426,23 +472,23 @@
     arrived(n_branch, gbranch.at[oth])
     head_grads(oth)
 
-    from_x = rows_all.at[x_to, 0]
-    arrived(n_m[1][0], from_x)
-    for k in range(1, ny):
-        send(n_m[1][k], from_x, from_x, dp=y_at(k, dx))
-
-    def second_hop():
-        arrived(n_g[1][0], rows_all.at[x_to, 1])
-        for k in range(1, ny):
-            block = rows_all.at[y_from(k, dx), 1]
-            arrived(n_g[0][k], block)
-            send(n_g[1][k], block, block, dp=x_to)
+
+    def second_hop(k):
+        block = rows_all.at[y_from(k, dx), 1]
+        arrived(n_g[0][k], block)
+        send(n_g[1][k], block, block, dp=x_to)
 
     acc_k[...] = jnp.zeros_like(acc_k)
     acc_v[...] = jnp.zeros_like(acc_v)
     for i in range(n_q):
+        if i == n_q - 2:
+            from_x = rows_all.at[x_to, 0]
+            arrived(n_m[1][0], from_x)
+            for k in range(1, ny):
+                send(n_m[1][k], from_x, from_x, dp=y_at(k, dx))
         if i == n_q - 1:
-            second_hop()
+            for k in range(1, ny):
+                second_hop(k)
         for pair in range(2):
             at = slice(pair * 128, pair * 128 + 128)
             q = rows_of(qs, i * per_q, per_q, pair)
@@ -519,150 +565,137 @@
 
     arrived(n_part, part_recv)
 
-    def grad_rows(b, total):
+    def grad_rows(b, carry):
         unit, inv_std = unit_norm(x_full[b, p].astype(F32))
         up = mixgrad[block_rows(b), :] + part_recv[b].astype(F32)
         grad = gresid[block_rows(b), :] + norm_back(up, unit, inv_std, gain_a)
         tgrad_send[b] = grad.astype(BF16)
-        return total + jnp.sum(up * unit, axis=0, keepdims=True)
-
-    gain_a_part = lax.fori_loop(0, nc, grad_rows, jnp.zeros((1, width), F32))
+        return carry
+
+    lax.fori_loop(0, nc, grad_rows, 0)
     n_tg = [number() for _ in range(nc)]
     for k in range(1, nc):
         to = chip_at(k)
         send(n_tg[k], tgrad_send.at[to], token_grad.at[c], grp=to * 2 + p)
     keep_tg = local(tgrad_send.at[c], token_grad.at[c])
 
-    tiles = 8 // nc
-    for j in range(8):
-        r, l = j // 4, j % 4
-        if ng >= 8 * (r + 1):
-            small_pay[j // tiles, j % tiles] = ctrl[r * 8 : r * 8 + 8, l * 128 : l * 128 + 128]
-        else:
-            small_pay[j // tiles, j % tiles] = jnp.zeros((8, 128), F32)
-            if ng > 8 * r:
-                small_pay[j // tiles, j % tiles, : ng - 8 * r] = ctrl[r * 8 : ng, l * 128 : l * 128 + 128]
-    for j in range(nc):
-        for l in range(4):
-            small_pay[j, tiles, l : l + 1] = gain_a_part[:, l * 128 : l * 128 + 128]
-            small_pay[j, tiles, 4 + l : 5 + l] = gain_m_part[:, l * 128 : l * 128 + 128]
-    n_s1 = [number() for _ in range(nc)]
-    for k in range(1, nc):
-        to = chip_at(k)
-        send(n_s1[k], small_pay.at[to], small_rs1.at[c], grp=to * 2 + p)
-    small_rs1[c] = small_pay[c]
-
-    def hidden_rows(x):
-        def body(f, carry):
-            at = pl.ds(pl.multiple_of(f * tile, tile), tile)
-            m_rows = rows_all[pl.ds(x * ny, ny), 0].reshape(ny * cols, width)
-            g_rows = rows_all[pl.ds(x * ny, ny), 1].reshape(ny * cols, width)
-            rows = pl.ds(pl.multiple_of(x * ny * cols, ny * cols), ny * cols)
-            silu, slope = silu_and_slope(mm(m_rows, win[:, at]))
-            hid[f, rows, :] = silu.astype(BF16)
-            gpr[f, rows, :] = (mm_nt(g_rows, wback[at, :]) * slope).astype(BF16)
-            return carry
-
-        lax.fori_loop(0, n_f, body, 0)
-
-    stores = []
-
-    def weight_grads(f):
-        slot = f % 2
-        if f >= 2:
-            for copy in stores[f - 2]:
+    n_rs2 = [[number() for _ in range(planes[r])] for r in range(n_red)]
+    n_ag1 = [[number() for _ in range(planes[r])] for r in range(n_red)]
+    n_ag2 = [[number() for _ in range(firsts[r])] for r in range(n_red)]
+    n_ag3 = [[number() for _ in range(firsts[r])] for r in range(n_red)]
+
+    def reduce_first():
+        for r in range(n_red):
+            for k in range(1, firsts[r]):
+                arrived(n_rs1[r][k], rs1.at[r, lax.rem(here_1[r] + firsts[r] - k, firsts[r])])
+            rs1[r, here_1[r]] = pay[r, here_1[r]]
+            total = rs1[r, 0].astype(F32)
+            for j in range(1, firsts[r]):
+                total = total + rs1[r, j].astype(F32)
+            red1[r] = total.astype(BF16)
+            for k in range(1, planes[r]):
+                to = lax.rem(here_2[r] + k, planes[r])
+                send(n_rs2[r][k], red1.at[r, to], rs2.at[r, here_2[r]], like=lambda r=r: red1.at[r, 0], **device_2[r](to))
+            rs2[r, here_2[r]] = red1[r, here_2[r]]
+
+    def reduce_second():
+        for r in range(n_red):
+            for k in range(1, planes[r]):
+                arrived(n_rs2[r][k], rs2.at[r, lax.rem(here_2[r] + planes[r] - k, planes[r])])
+            total = rs2[r, 0].astype(F32)
+            for j in range(1, planes[r]):
+                total = total + rs2[r, j].astype(F32)
+            red2[r] = total.astype(BF16)
+            for k in range(1, planes[r]):
+                to = lax.rem(here_2[r] + k, planes[r])
+                send(n_ag1[r][k], red2.at[r], ag1.at[r, here_2[r]], like=lambda r=r: red2.at[r], **device_2[r](to))
+            ag1[r, here_2[r]] = red2[r]
+
+    def gather_first():
+        for r in range(n_red):
+            for k in range(1, planes[r]):
+                arrived(n_ag1[r][k], ag1.at[r, lax.rem(here_2[r] + planes[r] - k, planes[r])])
+            place = reduced.at[p, r, here_1[r]]
+            for k in range(1, firsts[r]):
+                to = lax.rem(here_1[r] + k, firsts[r])
+                send(n_ag2[r][k], ag1.at[r], place, like=lambda r=r: ag1.at[r], **device_1(r, to))
+            send(n_ag3[r][0], ag1.at[r], place, like=lambda r=r: ag1.at[r], grp=sib)
+            keep_red(r).start()
+
+    red_sem = used[1]
+    store_sem = used[1] + n_red
+    used[1] += n_red + 2 * n_f
+
+    def keep_red(r):
+        return pltpu.make_async_copy(ag1.at[r], reduced.at[p, r, here_1[r]], local_sem.at[red_sem + r])
+
+    def hidden_rows(t, carry):
+        @pl.when(t == n_f)
+        def _():
+            small_step(1)
+            reduce_first()
+            for k in range(1, ny):
+                arrived(n_g[1][k], rows_all.at[y_from(k, 1 - dx), 1])
+                arrived(n_m[1][k], rows_all.at[y_from(k, 1 - dx), 0])
+            arrived(n_g[1][0], rows_all.at[x_to, 1])
+
+        @pl.when(t == n_f + n_f // 2)
+        def _():
+            reduce_second()
+
+        x = lax.rem(dx + t // n_f, 2)
+        f = lax.rem(t, n_f)
+        at = pl.ds(pl.multiple_of(f * tile, tile), tile)
+        m_rows = rows_all[pl.ds(x * ny, ny), 0].reshape(ny * cols, width)
+        g_rows = rows_all[pl.ds(x * ny, ny), 1].reshape(ny * cols, width)
+        rows = pl.ds(pl.multiple_of(x * ny * cols, ny * cols), ny * cols)
+        silu, slope = silu_and_slope(mm(m_rows, win[:, at]))
+        hid[f, rows, :] = silu.astype(BF16)
+        gpr[f, rows, :] = (mm_nt(g_rows, wback[at, :]) * slope).astype(BF16)
+        return carry
+
+    def stores(f):
+        slot = lax.rem(f, 2)
+        at = pl.ds(pl.multiple_of(f * tile, tile), tile)
+        return (
+            pltpu.make_async_copy(out_b.at[slot], grad_back.at[0, at, :], local_sem.at[store_sem + 2 * f]),
+            pltpu.make_async_copy(out_i.at[slot], grad_in.at[0, :, at], local_sem.at[store_sem + 2 * f + 1]),
+        )
+
+    def weight_grads(f, carry):
+        @pl.when(f == 1)
+        def _():
+            gather_first()
+
+        @pl.when(f >= 2)
+        def _():
+            for copy in stores(f - 2):
                 copy.wait()
+
+        slot = lax.rem(f, 2)
         m_rows = rows_all[:, 0].reshape(ndp * cols, width)
         g_rows = rows_all[:, 1].reshape(ndp * cols, width)
         out_b[slot] = mm_tn(hid[f], g_rows).astype(BF16)
         out_i[slot] = mm_tn(m_rows, gpr[f]).astype(BF16)
-        stores.append(
-            (
-                local(out_b.at[slot], grad_back.at[0, f * tile : (f + 1) * tile, :]),
-                local(out_i.at[slot], grad_in.at[0, :, f * tile : (f + 1) * tile]),
-            )
-        )
+        for copy in stores(f):
+            copy.start()
+        return carry
 
     for k in range(1, ny):
         arrived(n_m[0][k], rows_all.at[y_from(k, dx), 0])
-    hidden_rows(dx)
-
-    n_rs2 = [[number() for _ in range(planes[r])] for r in range(n_red)]
-    for r in range(n_red):
-        for k in range(1, firsts[r]):
-            arrived(n_rs1[r][k], rs1.at[r, lax.rem(here_1[r] + firsts[r] - k, firsts[r])])
-        rs1[r, here_1[r]] = pay[r, here_1[r]]
-        total = rs1[r, 0].astype(F32)
-        for j in range(1, firsts[r]):
-            total = total + rs1[r, j].astype(F32)
-        red1[r] = total.astype(BF16)
-        for k in range(1, planes[r]):
-            to = lax.rem(here_2[r] + k, planes[r])
-            send(n_rs2[r][k], red1.at[r, to], rs2.at[r, here_2[r]], **device_2[r](to))
-        rs2[r, here_2[r]] = red1[r, here_2[r]]
-    for k in range(1, nc):
-        arrived(n_s1[k], small_rs1.at[chip_from(k)])
-    small_sib[p] = small_rs1[...].sum(axis=0)
-    n_ss = number()
-    send(n_ss, small_sib.at[p], small_sib.at[p], grp=sib)
-
-    for k in range(1, ny):
-        arrived(n_g[1][k], rows_all.at[y_from(k, 1 - dx), 1])
-        arrived(n_m[1][k], rows_all.at[y_from(k, 1 - dx), 0])
-    hidden_rows(1 - dx)
-
-    n_ag1 = [[number() for _ in range(planes[r])] for r in range(n_red)]
-    for r in range(n_red):
-        for k in range(1, planes[r]):
-            arrived(n_rs2[r][k], rs2.at[r, lax.rem(here_2[r] + planes[r] - k, planes[r])])
-        total = rs2[r, 0].astype(F32)
-        for j in range(1, planes[r]):
-            total = total + rs2[r, j].astype(F32)
-        red2[r] = total.astype(BF16)
-        for k in range(1, planes[r]):
-            to = lax.rem(here_2[r] + k, planes[r])
-            send(n_ag1[r][k], red2.at[r], ag1.at[r, here_2[r]], **device_2[r](to))
-        ag1[r, here_2[r]] = red2[r]
-    arrived(n_ss, small_sib.at[oth])
-    small_dp[d] = small_sib[0] + small_sib[1]
-    n_sd = [number() for _ in range(ndp)]
-    for k in range(1, ndp):
-        send(n_sd[k], small_dp.at[d], small_dp.at[d], dp=lax.rem(d + k, ndp))
-
-    for f in range(n_f // 2):
-        weight_grads(f)
-
-    n_ag2 = [[number() for _ in range(firsts[r])] for r in range(n_red)]
-    n_ag3 = [[number() for _ in range(firsts[r])] for r in range(n_red)]
-    keep_red = []
-    for r in range(n_red):
-        for k in range(1, planes[r]):
-            arrived(n_ag1[r][k], ag1.at[r, lax.rem(here_2[r] + planes[r] - k, planes[r])])
-        place = reduced.at[p, r, here_1[r]]
-        for k in range(1, firsts[r]):
-            to = lax.rem(here_1[r] + k, firsts[r])
-            send(n_ag2[r][k], ag1.at[r], place, **device_1(r, to))
-        send(n_ag3[r][0], ag1.at[r], place, grp=sib)
-        keep_red.append(local(ag1.at[r], place))
-    for k in range(1, ndp):
-        arrived(n_sd[k], small_dp.at[lax.rem(d + ndp - k, ndp)])
-    small_fin[...] = small_dp[...].sum(axis=0)
-    n_sg = [number() for _ in range(nc)]
-    for k in range(1, nc):
-        send(n_sg[k], small_fin, small_out.at[c], grp=chip_at(k) * 2 + p)
+    small_step(0)
+    lax.fori_loop(0, 2 * n_f, hidden_rows, 0)
+    small_step(2)
     keep_small = local(small_fin, small_out.at[c])
-
-    for f in range(n_f // 2, n_f):
-        weight_grads(f)
-
+    lax.fori_loop(0, n_f, weight_grads, 0)
     for k in range(1, max(firsts)):
         for r in range(n_red):
             if k < firsts[r]:
                 place = reduced.at[p, r, lax.rem(here_1[r] + firsts[r] - k, firsts[r])]
                 arrived(n_ag2[r][k], place)
                 send(n_ag3[r][k], place, place, grp=sib)
-    for pair in stores[-2:]:
-        for copy in pair:
+    for f in (n_f - 2, n_f - 1):
+        for copy in stores(f):
             copy.wait()
     for k in range(1, nc):
         arrived(n_out[k], tokens_out.at[chip_from(k)])
@@ -671,16 +704,24 @@
     for r in range(n_red):
         for k in range(firsts[r]):
             arrived(n_ag3[r][k], reduced.at[oth, r, lax.rem(here_1[r] + firsts[r] - k, firsts[r])])
-    for copy in [keep_out, keep_tg, keep_small] + keep_red:
+    for copy in [keep_out, keep_tg, keep_small] + [keep_red(r) for r in range(n_red)]:
         copy.wait()
     for copy in started:
         copy.wait_send()
+    for n, like in in_loop:
+        ref = like()
+        pltpu.make_async_remote_copy(
+            src_ref=ref, dst_ref=ref, send_sem=send_sem.at[n], recv_sem=recv_sem.at[n],
+            device_id={"grp": sib}, device_id_type=MESH,
+        ).wait_send()
 
 
 def finish_kernel(
-    tokens_out, token_grad, reduced, small, grad_in, grad_back,
+    tokens_out, token_grad, reduced, small, grad_in, grad_back, w_qkv, gain_attn,
     out_tokens, out_tgrad, out_qkv, out_out, out_gain_a, out_gain_m, out_ctrl, out_in, out_back,
+    sums,
 ):
+    step, steps = pl.program_id(0), pl.num_programs(0)
     tiles = small.shape[1] - 1
     width = out_out.shape[2] * 2
     half = width // 2
@@ -690,17 +731,22 @@
     out_back[...] = grad_back[...].astype(F32)
     rows = out_qkv.shape[0]
     sub = reduced.shape[3] // 4
+    dots = jnp.zeros((rows, 1), F32)
     for p in range(2):
         for part in range(3):
-            at = part * width + p * half
-            out_qkv[:, at : at + half] = (
-                reduced[p, 0, 0, part * sub : (part + 1) * sub].reshape(rows, half).astype(F32)
-            )
+            at = slice(part * width + p * half, part * width + p * half + half)
+            grad = reduced[p, 0, 0, part * sub : (part + 1) * sub].reshape(rows, half).astype(F32)
+            out_qkv[:, at] = grad
+            dots = dots + jnp.sum(grad * w_qkv[:, at].astype(F32), axis=1, keepdims=True)
         out_out[p] = reduced[p, 0, 0, 3 * sub : 4 * sub].reshape(rows, half).astype(F32)
+    sums[pl.ds(pl.multiple_of(step * rows, rows), rows), :] = jnp.broadcast_to(dots, (rows, 128))
+
+    @pl.when(step == steps - 1)
+    def _():
+        out_gain_a[...] = sums[...].T[0:1] / gain_attn[...]
+
     for l in range(4):
-        at = slice(l * 128, l * 128 + 128)
-        out_gain_a[:, at] = small[0, tiles, l : l + 1]
-        out_gain_m[:, at] = small[0, tiles, 4 + l : 5 + l]
+        out_gain_m[:, l * 128 : l * 128 + 128] = small[0, tiles, l : l + 1]
     for j in range(8):
         out_ctrl[j // 4 * 8 : j // 4 * 8 + 8, j % 4 * 128 : j % 4 * 128 + 128] = small[j // tiles, j % tiles]
 
@@ -725,7 +771,7 @@
     scratch = [
         pltpu.SemaphoreType.DMA((SEMS,)),
         pltpu.SemaphoreType.DMA((SEMS,)),
-        pltpu.SemaphoreType.DMA((32,)),
+        pltpu.SemaphoreType.DMA((48,)),
         vm((nc, 2, BLOCK, width), BF16),
         vm((nc, BLOCK, width), BF16),
         vm((nc, 8, 128), jnp.int32),
@@ -827,6 +873,8 @@
             whole(small.shape),
             split(w_in.shape, 1),
             split(w_back.shape, 1),
+            split((width, 3 * width), 0),
+            whole((1, width)),
         ],
         out_specs=[
             split(tokens.shape, 0),
@@ -839,8 +887,9 @@
             split(w_in.shape, 1),
             split(w_back.shape, 1),
         ],
+        scratch_shapes=[vm((width, 128), F32)],
         name="finish",
-    )(tokens_out, token_grad, reduced, small, grad_in, grad_back)
+    )(tokens_out, token_grad, reduced, small, grad_in, grad_back, w_qkv, gain_attn.reshape(1, width))
     return (
         tokens_out,
         token_grad,

time: 133 us -> 129 us (0.970)
  Pallas kernels: 132 us -> 128 us
    pallas_call x1, Pallas kernels: 122 us -> 118 us  [on_device(): pl.pallas_call(functools.partial(block_kernel, ng, ndp, nx), out_shape=[j...]
    pallas_call x1, Pallas kernels: 9.38 us -> 10.7 us  [on_device(): pl.pallas_call(finish_kernel, grid=(steps,), out_shape=[jax.ShapeDtypeStr...]
where the time goes in v3:
time: 129 us
  Pallas kernels  128 us (99%)
    pallas_call x1, Pallas kernels, on_device(): pl.pallas_call(functools.partial(block_kernel, ng, ndp, nx), out_shape=[j...  118 us
    pallas_call x1, Pallas kernels, on_device(): pl.pallas_call(finish_kernel, grid=(steps,), out_shape=[jax.ShapeDtypeStr...  10.7 us

profile of v3, /device:TPU:1, one launch (start us, length us, event | category | flops | bytes accessed | tf_op | source)
XLA Modules:
  0.0 129.1 jit_solution(862926415010727564)
XLA Ops:
  0.6 117.5 %of_tokens_block.1 = (bf16[8,64,512]{2,1,0:T(8,128)(2,1)}, bf16[8,64,512]{2,1,0:T(8,128)(2,1)}, bf16[2,2,4,16,16,256]{5,4,3,2,1,0:T(8,128)(2,1)}, f32[8,2,8,128]...) custom-call(bf16[8,64,512]{2,1,0:T(8,128)(2,1)} %tokens.1, ...), custom_call_target="tpu_custom_call" | custom-call | tf_op jit(solution)/shard_map/of_tokens_block/pallas_call | solution.py:831
  118.2 10.7 %finish.1 = (bf16[8,64,512]{2,1,0:T(8,128)(2,1)}, f32[8,64,512]{2,1,0:T(8,128)}, f32[512,1536]{1,0:T(8,128)}, f32[2,256,512]{2,1,0:T(8,128)}, f32[1,512]{1,0:T(1...) custom-call(bf16[8,64,512]{2,1,0:T(8,128)(2,1)} %get-tuple-element.24.tokens_ou, ...), custom_call_target="tpu_custom_call" | custom-call | tf_op jit(solution)/shard_map/finish/pallas_call | solution.py:865

commit v4 on v3

--- a/solution.py
+++ b/solution.py
@@ -723,23 +723,31 @@
 ):
     step, steps = pl.program_id(0), pl.num_programs(0)
     tiles = small.shape[1] - 1
-    width = out_out.shape[2] * 2
+    width = out_out.shape[2]
     half = width // 2
     out_tokens[...] = tokens_out[...]
     out_tgrad[...] = token_grad[...].astype(F32)
     out_in[...] = grad_in[...].astype(F32)
     out_back[...] = grad_back[...].astype(F32)
-    rows = out_qkv.shape[0]
-    sub = reduced.shape[3] // 4
-    dots = jnp.zeros((rows, 1), F32)
-    for p in range(2):
-        for part in range(3):
-            at = slice(part * width + p * half, part * width + p * half + half)
-            grad = reduced[p, 0, 0, part * sub : (part + 1) * sub].reshape(rows, half).astype(F32)
-            out_qkv[:, at] = grad
-            dots = dots + jnp.sum(grad * w_qkv[:, at].astype(F32), axis=1, keepdims=True)
-        out_out[p] = reduced[p, 0, 0, 3 * sub : 4 * sub].reshape(rows, half).astype(F32)
-    sums[pl.ds(pl.multiple_of(step * rows, rows), rows), :] = jnp.broadcast_to(dots, (rows, 128))
+    chunks, sub = reduced.shape[2], reduced.shape[3] // 4
+    rows = out_qkv.shape[1] // chunks
+    for r in range(2):
+        for j in range(chunks):
+            here = slice(j * rows, (j + 1) * rows)
+            dots = jnp.zeros((rows, half), F32)
+            for p in range(2):
+                for part in range(3):
+                    at = slice(part * width + p * half, part * width + p * half + half)
+                    grad = reduced[p, r, j, part * sub : (part + 1) * sub].reshape(rows, half).astype(F32)
+                    out_qkv[r, here, at] = grad
+                    dots = dots + grad * w_qkv[r, here, at].astype(F32)
+                out_out[p, here, r * half : (r + 1) * half] = (
+                    reduced[p, r, j, 3 * sub : 4 * sub].reshape(rows, half).astype(F32)
+                )
+            first = r * half + (step * chunks + j) * rows
+            sums[pl.ds(pl.multiple_of(first, rows), rows), :] = jnp.broadcast_to(
+                jnp.sum(dots, axis=1, keepdims=True), (rows, 128)
+            )
 
     @pl.when(step == steps - 1)
     def _():
@@ -849,7 +857,7 @@
         tokens, cotangent, w_qkv, w_out.reshape(2, half, width), gain_attn.reshape(1, width),
         gain_mix.reshape(1, width), w_ctrl.T, w_in, w_back, prefix, group_ids,
     )
-    steps = 2 * n1
+    steps = n1 // 2
 
     def whole(shape):
         return pl.BlockSpec(shape, lambda s: (0,) * len(shape))
@@ -859,7 +867,7 @@
         return pl.BlockSpec(block, lambda s: tuple(s if i == axis else 0 for i in range(len(shape))))
 
     shapes = [
-        (tokens.shape, BF16), (tokens.shape, F32), ((width, 3 * width), F32), ((2, half, width), F32),
+        (tokens.shape, BF16), (tokens.shape, F32), ((2, half, 3 * width), F32), ((2, half, width), F32),
         ((1, width), F32), ((1, width), F32), ((16, width), F32), (w_in.shape, F32), (w_back.shape, F32),
     ]
     tokens_out, token_grad, grad_qkv, grad_out, gain_a, gain_m, ctrl, grad_in, grad_back = pl.pallas_call(
@@ -869,18 +877,18 @@
         in_specs=[
             split(tokens.shape, 0),
             split(tokens.shape, 0),
-            pl.BlockSpec((2, 1, 1, plane, 16, half), lambda s: (0, s // n1, s % n1, 0, 0, 0)),
+            pl.BlockSpec((2, 2, n1 // steps, plane, 16, half), lambda s: (0, 0, s, 0, 0, 0)),
             whole(small.shape),
             split(w_in.shape, 1),
             split(w_back.shape, 1),
-            split((width, 3 * width), 0),
+            split((2, half, 3 * width), 1),
             whole((1, width)),
         ],
         out_specs=[
             split(tokens.shape, 0),
             split(tokens.shape, 0),
-            split((width, 3 * width), 0),
-            pl.BlockSpec((2, half // n1, half), lambda s: (0, s % n1, s // n1)),
+            split((2, half, 3 * width), 1),
+            split((2, half, width), 1),
             whole((1, width)),
             whole((1, width)),
             whole((16, width)),
@@ -888,12 +896,16 @@
             split(w_back.shape, 1),
         ],
         scratch_shapes=[vm((width, 128), F32)],
+        compiler_params=pltpu.CompilerParams(vmem_limit_bytes=60 * 1024 * 1024),
         name="finish",
-    )(tokens_out, token_grad, reduced, small, grad_in, grad_back, w_qkv, gain_attn.reshape(1, width))
+    )(
+        tokens_out, token_grad, reduced, small, grad_in, grad_back,
+        w_qkv.reshape(2, half, 3 * width), gain_attn.reshape(1, width),
+    )
     return (
         tokens_out,
         token_grad,
-        grad_qkv,
+        grad_qkv.reshape(width, 3 * width),
         grad_out.reshape(width, width),
         gain_a.reshape(width),
         gain_m.reshape(width),

time: 129 us -> 127 us (0.984)
  Pallas kernels: 128 us -> 126 us
    pallas_call x1, Pallas kernels: 10.7 us -> 7.98 us  [on_device(): pl.pallas_call(finish_kernel, grid=(steps,), out_shape=[jax.ShapeDtypeStr...]
where the time goes in v4:
time: 127 us; the launch traced here: 126 us
  Pallas kernels  126 us (99%)
    pallas_call x1, Pallas kernels, on_device(): pl.pallas_call(functools.partial(block_kernel, ng, ndp, nx), out_shape=[j...  118 us
    pallas_call x1, Pallas kernels, on_device(): pl.pallas_call(finish_kernel, grid=(steps,), out_shape=[jax.ShapeDtypeStr...  7.98 us

profile of v4, /device:TPU:1, one launch (start us, length us, event | category | flops | bytes accessed | tf_op | source)
XLA Modules:
  0.0 126.3 jit_solution(18280487915532529424)
XLA Ops:
  0.6 117.5 %of_tokens_block.1 = (bf16[8,64,512]{2,1,0:T(8,128)(2,1)}, bf16[8,64,512]{2,1,0:T(8,128)(2,1)}, bf16[2,2,4,16,16,256]{5,4,3,2,1,0:T(8,128)(2,1)}, f32[8,2,8,128]...) custom-call(bf16[8,64,512]{2,1,0:T(8,128)(2,1)} %tokens.1, ...), custom_call_target="tpu_custom_call" | custom-call | tf_op jit(solution)/shard_map/of_tokens_block/pallas_call | solution.py:839
  118.2 8.0 %finish.1 = (bf16[8,64,512]{2,1,0:T(8,128)(2,1)}, f32[8,64,512]{2,1,0:T(8,128)}, f32[2,256,1536]{2,1,0:T(8,128)}, f32[2,256,512]{2,1,0:T(8,128)}, f32[1,512]{1,0...) custom-call(bf16[8,64,512]{2,1,0:T(8,128)(2,1)} %get-tuple-element.24.token, ...), custom_call_target="tpu_custom_call" | custom-call | tf_op jit(solution)/shard_map/finish/pallas_call | solution.py:873

commit v5 on v4

--- a/solution.py
+++ b/solution.py
@@ -639,7 +639,7 @@
                 arrived(n_m[1][k], rows_all.at[y_from(k, 1 - dx), 0])
             arrived(n_g[1][0], rows_all.at[x_to, 1])
 
-        @pl.when(t == n_f + n_f // 2)
+        @pl.when(t == n_f + n_f // 2 + 1)
         def _():
             reduce_second()
 

time: 127 us -> 126 us (level)
  no operation moved by 1% of the time
where the time goes in v5:
time: 126 us
  Pallas kernels  125 us (99%)
    pallas_call x1, Pallas kernels, on_device(): pl.pallas_call(functools.partial(block_kernel, ng, ndp, nx), out_shape=[j...  117 us
    pallas_call x1, Pallas kernels, on_device(): pl.pallas_call(finish_kernel, grid=(steps,), out_shape=[jax.ShapeDtypeStr...  7.98 us

profile of v5, /device:TPU:1, one launch (start us, length us, event | category | flops | bytes accessed | tf_op | source)
XLA Modules:
  0.0 125.7 jit_solution(5796274092829810223)
XLA Ops:
  0.6 116.9 %of_tokens_block.1 = (bf16[8,64,512]{2,1,0:T(8,128)(2,1)}, bf16[8,64,512]{2,1,0:T(8,128)(2,1)}, bf16[2,2,4,16,16,256]{5,4,3,2,1,0:T(8,128)(2,1)}, f32[8,2,8,128]...) custom-call(bf16[8,64,512]{2,1,0:T(8,128)(2,1)} %tokens.1, ...), custom_call_target="tpu_custom_call" | custom-call | tf_op jit(solution)/shard_map/of_tokens_block/pallas_call | solution.py:839
  117.6 8.0 %finish.1 = (bf16[8,64,512]{2,1,0:T(8,128)(2,1)}, f32[8,64,512]{2,1,0:T(8,128)}, f32[2,256,1536]{2,1,0:T(8,128)}, f32[2,256,512]{2,1,0:T(8,128)}, f32[1,512]{1,0...) custom-call(bf16[8,64,512]{2,1,0:T(8,128)(2,1)} %get-tuple-element.24.token, ...), custom_call_target="tpu_custom_call" | custom-call | tf_op jit(solution)/shard_map/finish/pallas_call | solution.py:873
